TPU v7x, 768 devices: a whole 4x8x12 slice. The times are simulated.
768 devices in a mesh: blk: 96 (over y, x, z_lo), grp: 8 (over z_hi, core).
Axes of the slice: x: 4, y: 8, z: 12 (z_hi: 4, z_lo: 3; z = z_hi * 3 + z_lo), core: 2. Of those that a mesh axis runs over, the one named last changes fastest.
Arguments:
- images: bfloat16 [1536, 3, 1024], P(('blk', 'grp')), may hold values from -10 to 10
Outputs:
- kernel_window: float32 [1536, 5, 16], P(('blk', 'grp'))
All inputs are finite; a program needn't handle non-finite values.
Results may differ from a plain program's by a relative error of at most 0.0003.
Values may be sent and summed in bfloat16 or wider, within the bound.
No kernel may reach another device: no remote copies, remote signals or barrier semaphores. Data moves between devices by JAX's collectives and lax.ppermute only.
A program may use at most 32 MiB of HBM per device.

v0:
```python
import functools

import jax
import jax.numpy as jnp
import numpy as np
from jax import lax
from jax.experimental import pallas as pl
from jax.experimental.pallas import tpu as pltpu
from jax.sharding import PartitionSpec as P

SIDE = 32
LAYERS = 3
CHIP_ROWS = 4
GRP = 8
bias_var = 0.1

TAIL = (
    0.3001054023535799,
    0.015007729426877447,
    0.0023848543747712397,
    0.0006623160561359935,
    -2.0047167192458316e-05,
    0.00016959256815365074,
)


def stencil_weights():
    lane = np.arange(128)
    row, col = lane // SIDE, lane % SIDE
    near = np.abs(col[:, None] - col[None, :]) <= 1
    inner = near & (np.abs(row[:, None] - row[None, :]) <= 1)
    cross = near & (
        ((row[:, None] == 3) & (row[None, :] == 0)) | ((row[:, None] == 0) & (row[None, :] == 3))
    )
    half = np.concatenate([inner, cross], 1).astype(np.float32)
    return np.concatenate([half, half], 0)


def split(x):
    high = x.astype(jnp.bfloat16)
    low = (x - high.astype(jnp.float32)).astype(jnp.bfloat16)
    return high, low


def stencil_sum(maps, weights, from_above, from_below):
    count = maps.shape[0]
    high, low = split(maps.reshape(count * 8, 128))
    both = jnp.dot(
        jnp.concatenate([high, low], 1), weights, preferred_element_type=jnp.float32
    )
    inner = both[:, :128].reshape(count, 8, 128)
    cross = both[:, 128:].reshape(count, 8, 128)
    down = pltpu.roll(cross, 1, 1)
    up = pltpu.roll(cross, 7, 1)
    return inner + jnp.where(from_above, down, jnp.where(from_below, up, 0.0))


def masks():
    sub = lax.broadcasted_iota(jnp.int32, (1, 8, 128), 1)
    lane = lax.broadcasted_iota(jnp.int32, (1, 8, 128), 2)
    return (lane < SIDE) & (sub >= 1), (lane >= 3 * SIDE) & (sub <= 6)


def load_images(ref, first, count):
    pairs = ref[pl.ds(first, count)].astype(jnp.float32)
    return pairs.reshape(count * 2, 3, 8, 128)


def variance_maps(channels, weights, above, below):
    current = jnp.sum(channels * channels, 1) * (1.0 / 27.0)
    out = []
    for layer in range(LAYERS):
        if layer:
            current = current * (1.0 / 9.0)
        current = stencil_sum(current, weights, above, below) + bias_var
        inverse = lax.rsqrt(current)
        out.append((inverse, current * inverse))
    return out


def relu_over_scale(ratio):
    gap = 1.0 - jnp.minimum(jnp.abs(ratio), 1.0)
    poly = jnp.float32(TAIL[-1])
    for coefficient in TAIL[-2::-1]:
        poly = poly * gap + jnp.float32(coefficient)
    return jnp.clip(ratio, 0.0, 1.0) + gap * gap * lax.rsqrt(jnp.maximum(gap, 1e-30)) * poly


def fold(maps):
    sub = lax.broadcasted_iota(jnp.int32, (1, 8, 128), 1)
    for width in (4, 2, 1):
        first, second = maps[:width], maps[width:]
        low = (sub % (2 * width)) < width
        kept = jnp.where(low, first, second)
        if width == 4:
            other = pltpu.roll(jnp.where(low, second, first), 4, 1)
        else:
            other = jnp.where(low, pltpu.roll(first, 8 - width, 1), pltpu.roll(second, width, 1))
        maps = kept + other
    return maps[0]


def lane_sums(rows):
    ones = jnp.ones((8, 256), jnp.bfloat16)
    return lax.dot_general(
        ones,
        jnp.concatenate(split(rows), 1),
        (((1,), (1,)), ((), ())),
        preferred_element_type=jnp.float32,
    )


def pair_tile(row_refs, columns, weights, above, below):
    count = columns.shape[0]
    column_var = variance_maps(columns, weights, above, below)
    tile = jnp.zeros((8, 128), jnp.float32)
    sub = lax.broadcasted_iota(jnp.int32, (8, 128), 0)
    for row in range(CHIP_ROWS):
        folded = []
        for group in range(0, count, 8):
            part = slice(group, group + 8)
            product = row_refs[row, 0][None] * columns[part, 0]
            for channel in (1, 2):
                product = product + row_refs[row, channel][None] * columns[part, channel]
            for layer in range(LAYERS):
                cov = stencil_sum(product, weights, above, below) + bias_var
                inverse, scale = column_var[layer]
                ratio = cov * (row_refs[row, 3 + layer][None] * inverse[part])
                product = (row_refs[row, 6 + layer][None] * scale[part]) * relu_over_scale(ratio)
            folded.append(fold(product))
        sums = lane_sums(jnp.concatenate(folded, 0))
        sums = jnp.concatenate([sums, jnp.zeros((8, 128 - count), jnp.float32)], 1)
        tile = jnp.where(sub == row, sums, tile)
    return tile


def own_kernel(block_ref, weights_ref, tile_ref, rows_ref):
    place = lax.axis_index("grp")
    chip, core = place // 2, place % 2
    weights = weights_ref[...]
    above, below = masks()
    rows = load_images(block_ref, 2 * chip, 2)
    row_var = variance_maps(rows, weights, above, below)
    for channel in range(3):
        rows_ref[:, channel] = rows[:, channel] * (1.0 / 27.0)
    for layer in range(LAYERS):
        inverse, scale = row_var[layer]
        rows_ref[:, 3 + layer] = inverse
        rows_ref[:, 6 + layer] = scale * (1.0 / 9.0 if layer < LAYERS - 1 else 1.0 / 1024.0)
    columns = load_images(block_ref, 4 * core, 4)
    tile_ref[...] = pair_tile(rows_ref, columns, weights, above, below)


def visitor_kernel(rows_ref, block_ref, weights_ref, tile_ref):
    above, below = masks()
    columns = load_images(block_ref, 0, GRP)
    tile_ref[...] = pair_tile(rows_ref, columns, weights_ref[...], above, below)


def last_kernel(rows_ref, block_ref, weights_ref, own_ref, near_ref, tile_ref):
    above, below = masks()
    columns = load_images(block_ref, 0, GRP)
    far = pair_tile(rows_ref, columns, weights_ref[...], above, below)
    tile_ref[...] = own_ref[...] + pltpu.roll(near_ref[...], 8, 1) + pltpu.roll(far, 24, 1)


def call(body, outs, pairs):
    return pl.pallas_call(
        body,
        out_shape=outs,
        compiler_params=pltpu.CompilerParams(vmem_limit_bytes=32 * 1024 * 1024),
        cost_estimate=pl.CostEstimate(
            flops=pairs * 3 * 1024 * 512, bytes_accessed=1 << 20, transcendentals=pairs * 3 * 1024
        ),
    )


def by_core(block, distance, blocks):
    route = []
    for block_index in range(blocks):
        for place in range(GRP):
            source = (block_index + (distance if place % 2 else -distance)) % blocks
            route.append((source * GRP + place, block_index * GRP + place))
    return lax.ppermute(block, ("blk", "grp"), route)


def per_device(images):
    blocks = lax.axis_size("blk")
    weights = jnp.asarray(stencil_weights(), jnp.bfloat16)
    mine = images.reshape(1, 48, 128)
    block = lax.all_gather(mine, "grp", axis=0, tiled=True)
    near = by_core(block, 1, blocks)
    far = by_core(block, 2, blocks)
    tile = jax.ShapeDtypeStruct((8, 128), jnp.float32)
    rows = jax.ShapeDtypeStruct((CHIP_ROWS, 9, 8, 128), jnp.float32)
    own_tile, row_maps = call(own_kernel, (tile, rows), 32)(block, weights)
    near_tile = call(visitor_kernel, tile, 64)(row_maps, near, weights)
    packed = call(last_kernel, tile, 64)(row_maps, far, weights, own_tile, near_tile)
    chips = [[2 * chip, 2 * chip + 1] for chip in range(GRP // 2)]
    both = lax.all_gather(packed, "grp", axis=0, axis_index_groups=chips)
    core = lax.axis_index("grp") % 2
    mine = lax.dynamic_slice(both, (0, 2 * core, 0), (2, 2, 40))
    low, high = mine[0], mine[1]
    return jnp.stack(
        [
            low[:, 24:40],
            low[:, 8:24],
            jnp.concatenate([low[:, :8], high[:, :8]], 1),
            high[:, 8:24],
            high[:, 24:40],
        ],
        1,
    )


def solution(mesh):
    in_specs = (P(("blk", "grp"), None, None),)
    out_specs = P(("blk", "grp"), None, None)
    return jax.shard_map(
        per_device, mesh=mesh, in_specs=in_specs, out_specs=out_specs, check_vma=False
    )
```

profile of v0, /device:TPU:1, one launch (start us, length us, event | category | flops | bytes accessed | tf_op | source)
XLA Modules:
  0.0 49.6 jit_solution(7409923474516446752)
XLA Ops:
  0.0 0.0 copy-start
  0.0 0.7 %copy.5 = bf16[2,3,1024]{2,1,0:T(4,128)(2,1)S(1)} copy(bf16[2,3,1024]{2,0,1:T(2,128)(2,1)} %param.2) | data formatting | bytes 24576 | tf_op args[0]
  0.8 26.7 %all_gather.9.block_ref = bf16[8,48,128]{2,1,0:T(8,128)(2,1)S(1)} all-gather(bf16[1,48,128]{2,1,0:T(8,128)(2,1)S(1)} %reshape.3), channel_id=1, replica_groups=mesh['blk'=96,'grp'=8] {'grp'}, dimensions={0}, use_global_device_ids=true | all-gather | bytes 110592 | tf_op jit(solution)/shard_map/all_gather | solution.py:191
  27.5 8.9 %collective-permute-start.1 = (bf16[8,48,128]{2,1,0:T(8,128)(2,1)S(1)}, bf16[8,48,128]{2,1,0:T(8,128)(2,1)S(1)}, u32[]{:S(2)}, u32[]{:S(2)}) collective-permute-start(bf16[8,48,128]{2,1,0:T(8,128)(2,1)S(1)} %all_gather.9.block_ref), channel_id=1, source_target_pairs={{760,0},{9,1},{762,2},{11,3},{764,4},{13,5},{766,6},{15,7},{0,8},{... | collective-permute-start | bytes 294920 | tf_op jit(solution)/shard_map/ppermute | solution.py:184
  36.4 1.9 %collective-permute-start = (bf16[8,48,128]{2,1,0:T(8,128)(2,1)S(1)}, bf16[8,48,128]{2,1,0:T(8,128)(2,1)S(1)}, u32[]{:S(2)}, u32[]{:S(2)}) collective-permute-start(bf16[8,48,128]{2,1,0:T(8,128)(2,1)S(1)} %all_gather.9.block_ref), channel_id=1, source_target_pairs={{752,0},{17,1},{754,2},{19,3},{756,4},{21,5},{758,6},{23,7},{760,8... | collective-permute-start | bytes 294920 | tf_op jit(solution)/shard_map/ppermute | solution.py:184
  38.3 0.0 copy-done
  38.3 2.4 %shard_map.28 = (f32[8,128]{1,0:T(8,128)S(1)}, f32[4,9,8,128]{3,2,1,0:T(8,128)S(1)}) custom-call(bf16[8,48,128]{2,1,0:T(8,128)(2,1)S(1)} %all_gather.9.block_ref, bf16[256,256]{1,0:T(8,128)(2,1)S(1)} %copy-done), custom_call_target="tpu_custom_call" | custom-call | flops 50331648 | bytes 1048576 | tf_op jit(solution)/shard_map/pallas_call | solution.py:196
  40.7 0.0 collective-permute-done.1.block_ref
  40.7 2.7 %shard_map.29.near_ref = f32[8,128]{1,0:T(8,128)S(1)} custom-call(f32[4,9,8,128]{3,2,1,0:T(8,128)S(1)} %get-tuple-element.7.rows_ref, bf16[8,48,128]{2,1,0:T(8,128)(2,1)S(1)} %collective-permute-done.1.block_ref, bf16[256,256]{1,0:T(8,128)(2,1)S(1)} %copy-done), custom_call_target="tpu_custom_call" | custom-call | flops 100663296 | bytes 1048576 | tf_op jit(solution)/shard_map/pallas_call | solution.py:197
  43.5 0.0 collective-permute-done.block_ref
  43.5 2.8 %shard_map.30 = f32[8,128]{1,0:T(8,128)S(1)} custom-call(f32[4,9,8,128]{3,2,1,0:T(8,128)S(1)} %get-tuple-element.7.rows_ref, bf16[8,48,128]{2,1,0:T(8,128)(2,1)S(1)} %collective-permute-done.block_ref, bf16[256,256]{1,0:T(8,128)(2,1)S(1)} %copy-done, f32[8,128]{1,0:T(8,128)S(1)} %get-tuple-element.8.own_ref, f32[8,128]{1,0:T(8,128)S(1)} %shard_map.29.near_ref), custom_call_target="tpu_custom_call" | custom-call | flops 100663296 | bytes 1048576 | tf_op jit(solution)/shard_map/pallas_call | solution.py:198
  46.3 1.8 %all-gather = f32[16,128]{1,0:T(8,128)S(1)} all-gather(f32[8,128]{1,0:T(8,128)S(1)} %shard_map.30), channel_id=2, replica_groups={{0,1},{2,3},{4,5},{6,7},{8,9},{10,11},{12,13},{14,15},{16,17},{18,19},{..., dimensions={0}, use_global_device_ids=true | all-gather | bytes 12288 | tf_op jit(solution)/shard_map/all_gather | solution.py:200
  48.1 0.1 constant_dynamic-update-slice_fusion.4
  48.1 0.1 constant_dynamic-update-slice_fusion.3
  48.2 0.1 constant_dynamic-update-slice_fusion.2
  48.3 0.1 constant_dynamic-update-slice_fusion.1
  48.4 0.0 copy-start.1
  48.4 0.6 %copy-done.1 = f32[2,5,16]{2,0,1:T(2,128)} copy-done((f32[2,5,16]{2,0,1:T(2,128)}, f32[2,5,16]{2,0,1:T(2,128)S(1)}, u32[]{:S(2)}) %copy-start.1) | copy-done | bytes 664
  49.0 0.6 %constant_dynamic-update-slice_fusion = f32[2,5,16]{2,0,1:T(2,128)} fusion(f32[2,5,16]{2,0,1:T(2,128)} %copy-done.1, f32[2,40]{1,0:T(2,128)S(1)} %get-tuple-element.9), kind=kLoop, calls=%fused_computation | loop fusion | bytes 1152 | tf_op jit(solution)/shard_map/stack | solution.py:204
  (2 shorter events, 0.0 us)
Async XLA Ops:
  0.0 38.3 %copy-start = (bf16[256,256]{1,0:T(8,128)(2,1)S(1)}, bf16[256,256]{1,0:T(8,128)(2,1)}, u32[]{:S(2)}) copy-start(bf16[256,256]{1,0:T(8,128)(2,1)} %constant.22.clone.weights_ref) | copy-start | bytes 393220
  27.5 13.3 %collective-permute-start.1 = (bf16[8,48,128]{2,1,0:T(8,128)(2,1)S(1)}, bf16[8,48,128]{2,1,0:T(8,128)(2,1)S(1)}, u32[]{:S(2)}, u32[]{:S(2)}) collective-permute-start(bf16[8,48,128]{2,1,0:T(8,128)(2,1)S(1)} %all_gather.9.block_ref), channel_id=1, source_target_pairs={{760,0},{9,1},{762,2},{11,3},{764,4},{13,5},{766,6},{15,7},{0,8},{... | collective-permute-start | bytes 294920 | tf_op jit(solution)/shard_map/ppermute | solution.py:184
  36.4 7.1 %collective-permute-start = (bf16[8,48,128]{2,1,0:T(8,128)(2,1)S(1)}, bf16[8,48,128]{2,1,0:T(8,128)(2,1)S(1)}, u32[]{:S(2)}, u32[]{:S(2)}) collective-permute-start(bf16[8,48,128]{2,1,0:T(8,128)(2,1)S(1)} %all_gather.9.block_ref), channel_id=1, source_target_pairs={{752,0},{17,1},{754,2},{19,3},{756,4},{21,5},{758,6},{23,7},{760,8... | collective-permute-start | bytes 294920 | tf_op jit(solution)/shard_map/ppermute | solution.py:184
  48.4 0.6 %copy-start.1 = (f32[2,5,16]{2,0,1:T(2,128)}, f32[2,5,16]{2,0,1:T(2,128)S(1)}, u32[]{:S(2)}) copy-start(f32[2,5,16]{2,0,1:T(2,128)S(1)} %constant_dynamic-update-slice_fusion.1) | copy-start | bytes 1924
where the time goes:
time: 49.8 us; the launch traced here: 49.6 us
  blocking collectives  28.5 us (57%)
  starting transfers between devices  10.8 us (22%)
  Pallas kernels  7.93 us (16%)
  local copies, waits for them, and re-layouts  2.24 us (4%)
    all_gather x1, blocking collectives, per_device(): block = lax.all_gather(mine, 'grp', axis=0, tiled=True)  26.7 us
    ppermute x2, starting transfers between devices, by_core(): return lax.ppermute(block, ('blk', 'grp'), route)  10.8 us
    pallas_call x1, Pallas kernels, per_device(): call(last_kernel, tile, 64)(row_maps, far, weights, own_tile, near_tile)  2.79 us
    pallas_call x1, Pallas kernels, per_device(): near_tile = call(visitor_kernel, tile, 64)(row_maps, near, weights)  2.72 us
    pallas_call x1, Pallas kernels, per_device(): own_tile, row_maps = call(own_kernel, (tile, rows), 32)(block, weights)  2.42 us
    all_gather x1, blocking collectives, per_device(): both = lax.all_gather(packed, 'grp', axis=0, axis_index_groups=chips)  1.79 us
    unnamed x8, local copies, waits for them, and re-layouts  1.57 us
  transfers between devices with their start and end apart: 2, of which 0 were waited for; matrix products, arithmetic and copies ran while one was open for 0% of the time, Pallas kernels for 10%

commit v1 on v0

v1 whole, which is shorter than its diff:
```python
import functools

import jax
import jax.numpy as jnp
import numpy as np
from jax import lax
from jax.experimental import pallas as pl
from jax.experimental.pallas import tpu as pltpu
from jax.sharding import PartitionSpec as P

SIDE = 32
LAYERS = 3
CHIP_ROWS = 4
GRP = 8
bias_var = 0.1

TAIL = (
    0.3001054023535799,
    0.015007729426877447,
    0.0023848543747712397,
    0.0006623160561359935,
    -2.0047167192458316e-05,
    0.00016959256815365074,
)


def stencil_weights():
    lane = np.arange(128)
    row, col = lane // SIDE, lane % SIDE
    near = np.abs(col[:, None] - col[None, :]) <= 1
    inner = near & (np.abs(row[:, None] - row[None, :]) <= 1)
    cross = near & (
        ((row[:, None] == 3) & (row[None, :] == 0)) | ((row[:, None] == 0) & (row[None, :] == 3))
    )
    half = np.concatenate([inner, cross], 1).astype(np.float32)
    return np.concatenate([half, half], 0)


def split(x):
    high = x.astype(jnp.bfloat16)
    low = (x - high.astype(jnp.float32)).astype(jnp.bfloat16)
    return high, low


def stencil_sum(maps, weights, from_above, from_below):
    count = maps.shape[0]
    high, low = split(maps.reshape(count * 8, 128))
    both = jnp.dot(
        jnp.concatenate([high, low], 1), weights, preferred_element_type=jnp.float32
    )
    inner = both[:, :128].reshape(count, 8, 128)
    cross = both[:, 128:].reshape(count, 8, 128)
    down = pltpu.roll(cross, 1, 1)
    up = pltpu.roll(cross, 7, 1)
    return inner + jnp.where(from_above, down, jnp.where(from_below, up, 0.0))


def masks():
    sub = lax.broadcasted_iota(jnp.int32, (1, 8, 128), 1)
    lane = lax.broadcasted_iota(jnp.int32, (1, 8, 128), 2)
    return (lane < SIDE) & (sub >= 1), (lane >= 3 * SIDE) & (sub <= 6)


def load_images(ref, places, spread, slot=0):
    images = []
    for place in places:
        spread[pl.ds(slot * 48, 48)] = ref[place].astype(jnp.float32)
        for image in range(2):
            images += [
                spread[pl.ds(slot * 48 + channel * 16 + image, 8, stride=2)]
                for channel in range(3)
            ]
        slot += 1
    return jnp.stack(images, 0).reshape(2 * len(places), 3, 8, 128)


def relu_over_scale(ratio):
    gap = 1.0 - jnp.minimum(jnp.abs(ratio), 1.0)
    poly = jnp.float32(TAIL[-1])
    for coefficient in TAIL[-2::-1]:
        poly = poly * gap + jnp.float32(coefficient)
    return jnp.clip(ratio, 0.0, 1.0) + gap * gap * lax.rsqrt(jnp.maximum(gap, 1e-30)) * poly


def fold(maps):
    sub = lax.broadcasted_iota(jnp.int32, (1, 8, 128), 1)
    for width in (4, 2, 1):
        first, second = maps[:width], maps[width:]
        low = (sub % (2 * width)) < width
        kept = jnp.where(low, first, second)
        if width == 4:
            other = pltpu.roll(jnp.where(low, second, first), 4, 1)
        else:
            other = jnp.where(low, pltpu.roll(first, 8 - width, 1), pltpu.roll(second, width, 1))
        maps = kept + other
    return maps[0]


def lane_sums(rows):
    ones = jnp.ones((8, 256), jnp.bfloat16)
    return lax.dot_general(
        ones,
        jnp.concatenate(split(rows), 1),
        (((1,), (1,)), ((), ())),
        preferred_element_type=jnp.float32,
    )


def squares(channels):
    return jnp.sum(channels * channels, 1) * (1.0 / 27.0)


def pair_tile(row_channels, columns, weights, row_maps=None):
    above, below = masks()
    count = columns.shape[0]
    pairs = CHIP_ROWS * count
    products = []
    for row in range(CHIP_ROWS):
        terms = (row_channels[row] * (1.0 / 27.0))[None] * columns
        products.append(terms[:, 0] + terms[:, 1] + terms[:, 2])
    maps = products + [squares(columns)]
    if row_maps is None:
        maps.append(squares(row_channels))
    made = []
    for layer in range(LAYERS):
        sums = stencil_sum(jnp.concatenate(maps, 0), weights, above, below) + bias_var
        variance = sums[pairs:]
        inverse = lax.rsqrt(variance)
        scale = variance * inverse
        if row_maps is None:
            factor = 1.0 / 9.0 if layer < LAYERS - 1 else 1.0 / 1024.0
            row_inverse, row_scale = inverse[count:], scale[count:] * factor
            made.append((row_inverse, row_scale))
        else:
            row_inverse, row_scale = row_maps[layer]
        maps = []
        for row in range(CHIP_ROWS):
            part = sums[row * count : (row + 1) * count]
            ratio = part * (row_inverse[row][None] * inverse[:count])
            maps.append((row_scale[row][None] * scale[:count]) * relu_over_scale(ratio))
        if layer < LAYERS - 1:
            maps.append(variance * (1.0 / 9.0))
    tile = jnp.zeros((8, 128), jnp.float32)
    sub = lax.broadcasted_iota(jnp.int32, (8, 128), 0)
    for row in range(CHIP_ROWS):
        folded = [fold(maps[row][group : group + 8]) for group in range(0, count, 8)]
        sums = lane_sums(jnp.concatenate(folded, 0))
        sums = jnp.concatenate([sums, jnp.zeros((8, 128 - count), jnp.float32)], 1)
        tile = jnp.where(sub == row, sums, tile)
    return tile, made


def own_kernel(block_ref, weights_ref, tile_ref, rows_ref, spread):
    place = lax.axis_index("grp")
    chip, core = place // 2, place % 2
    at = 2 * jnp.where(chip == 0, 0, jnp.where(chip == 1, 2, jnp.where(chip == 2, 3, 1)))
    rows = load_images(block_ref, (at, at + 1), spread)
    first, second = jnp.where(core == 0, 0, 6), jnp.where(core == 0, 4, 2)
    columns = load_images(block_ref, (first, first + 1, second, second + 1), spread, 2)
    tile, row_maps = pair_tile(rows, columns, weights_ref[...])
    tile_ref[...] = tile
    rows_ref[:, :3] = rows
    for layer in range(LAYERS):
        rows_ref[:, 3 + layer] = row_maps[layer][0]
        rows_ref[:, 6 + layer] = row_maps[layer][1]


def visitor_tile(rows_ref, block_ref, weights_ref, spread):
    columns = load_images(block_ref, (0, 1, 4, 5, 6, 7, 2, 3), spread)
    row_maps = [(rows_ref[:, 3 + layer], rows_ref[:, 6 + layer]) for layer in range(LAYERS)]
    return pair_tile(rows_ref[:, :3], columns, weights_ref[...], row_maps)[0]


def visitor_kernel(rows_ref, block_ref, weights_ref, tile_ref, spread):
    tile_ref[...] = visitor_tile(rows_ref, block_ref, weights_ref, spread)


def last_kernel(rows_ref, block_ref, weights_ref, own_ref, inside_ref, tile_ref, spread):
    cross = visitor_tile(rows_ref, block_ref, weights_ref, spread)
    tile_ref[...] = own_ref[...] + pltpu.roll(inside_ref[...], 8, 1) + pltpu.roll(cross, 24, 1)


def assemble_kernel(both_ref, out_ref):
    level = lax.axis_index("blk") % 3
    core = lax.axis_index("grp") % 2
    low, high = [jnp.where(core == 0, both_ref[at, :2], both_ref[at, 2:4]) for at in (0, 1)]
    low_inside, high_inside = low[:, 8:24], high[:, 8:24]
    low_cross, high_cross = low[:, 24:40], high[:, 24:40]
    out_ref[0] = jnp.where(level == 2, high_inside, low_cross)
    out_ref[1] = jnp.where(level == 0, high_cross, low_inside)
    out_ref[2] = jnp.concatenate([low[:, :8], high[:, :8]], 1)
    out_ref[3] = jnp.where(level == 2, low_cross, high_inside)
    out_ref[4] = jnp.where(level == 0, low_inside, high_cross)


def call(body, outs, pairs, places):
    return pl.pallas_call(
        body,
        out_shape=outs,
        scratch_shapes=[pltpu.VMEM((places * 48, 128), jnp.float32)] if places else [],
        compiler_params=pltpu.CompilerParams(vmem_limit_bytes=32 * 1024 * 1024),
        cost_estimate=pl.CostEstimate(
            flops=pairs * 3 * 1024 * 512, bytes_accessed=1 << 20, transcendentals=pairs * 3 * 1024
        ),
    )


def routes():
    lines = 32

    def device(line, level, chip, core):
        return ((line % lines) * 3 + level) * GRP + chip * 2 + core

    across = {
        (0, 0): (-1, 1),
        (0, 1): (-1, 2),
        (1, 0): (-1, 2),
        (1, 1): (1, 0),
        (2, 0): (1, 0),
        (2, 1): (1, 1),
    }
    cross, inside, used = [], [], {}
    for line in range(lines):
        for chip in range(GRP // 2):
            for level in range(3):
                for core in (0, 1):
                    here = device(line, level, chip, core)
                    step, source = across[level, core]
                    sender = (line + step) % lines, source, chip
                    turn = used.get(sender, 0)
                    used[sender] = turn + 1
                    cross.append((device(*sender, turn), here))
                    source = (level + (1 if core else 2)) % 3
                    inside.append((device(line, source, chip, 1 - core), here))
    return cross, inside


def per_device(images):
    weights = jnp.asarray(stencil_weights(), jnp.bfloat16)
    mine = images.reshape(2, 3, 8, 128).transpose(1, 2, 0, 3).reshape(1, 48, 128)
    halves = [[0, 1, 6, 7], [2, 3, 4, 5]]
    pairs = [[0, 2], [1, 3], [6, 4], [7, 5]]
    block = lax.all_gather(mine, "grp", axis=0, tiled=True, axis_index_groups=halves)
    block = lax.all_gather(block, "grp", axis=0, tiled=True, axis_index_groups=pairs)
    cross_route, inside_route = routes()
    inside = lax.ppermute(block, ("blk", "grp"), inside_route)
    cross = lax.ppermute(block, ("blk", "grp"), cross_route)
    tile = jax.ShapeDtypeStruct((8, 128), jnp.float32)
    rows = jax.ShapeDtypeStruct((CHIP_ROWS, 9, 8, 128), jnp.float32)
    own_tile, row_maps = call(own_kernel, (tile, rows), 32, 6)(block, weights)
    inside_tile = call(visitor_kernel, tile, 64, GRP)(row_maps, inside, weights)
    packed = call(last_kernel, tile, 64, GRP)(row_maps, cross, weights, own_tile, inside_tile)
    chips = [[2 * chip, 2 * chip + 1] for chip in range(GRP // 2)]
    both = lax.all_gather(packed, "grp", axis=0, axis_index_groups=chips)
    result = call(assemble_kernel, jax.ShapeDtypeStruct((5, 2, 16), jnp.float32), 0, 0)(both)
    return jnp.transpose(result, (1, 0, 2))


def solution(mesh):
    in_specs = (P(("blk", "grp"), None, None),)
    out_specs = P(("blk", "grp"), None, None)
    return jax.shard_map(
        per_device, mesh=mesh, in_specs=in_specs, out_specs=out_specs, check_vma=False
    )
```

time: 49.8 us -> 45.2 us (0.908)
  Pallas kernels: 7.93 us -> 4.72 us
  local copies, waits for them, and re-layouts: 2.24 us -> 0.01 us
  starting transfers between devices: 10.8 us -> 12.5 us
  blocking collectives: 28.5 us -> 27.4 us
    pallas_call x3 -> x4, Pallas kernels: 7.93 us -> 4.72 us  [the longest x1 1.5 us: per_device(): call(last_kernel, tile, 64, GRP)]
    all_gather x1 -> x2, blocking collectives: 26.7 us -> 24.3 us  [the longest x1 18.9 us: per_device(): lax.all_gather(mine, 'grp', axis=0, tiled=True, axis_index_groups=halves)]
    ppermute x2, starting transfers between devices: 10.8 us -> 12.5 us  [the longest x1 8.26 us: per_device(): cross = lax.ppermute(block, ('blk', 'grp'), cross_route)]
    unnamed x8 -> x2, local copies, waits for them, and re-layouts: 1.57 us -> 0.01 us
    all_gather x1, blocking collectives: 1.79 us -> 3.14 us  [per_device(): both = lax.all_gather(packed, 'grp', axis=0, axis_index_groups=chips)]
    another operation x1 -> x0, local copies, waits for them, and re-layouts: 0.63 us -> none  [per_device(): jnp.stack([low[:, 24:40], low[:, 8:24], jnp.concatenate([low[:, :8], high...]
  transfers between devices with their start and end apart: 2 -> 2, of which waited for: 0 -> 1; matrix products, arithmetic and copies ran while one was open for 0% -> 0% of each run, Pallas kernels for 10% -> 5%
where the time goes in v1:
time: 45.2 us; the launch traced here: 45.1 us
  blocking collectives  27.4 us (61%)
  starting transfers between devices  12.5 us (28%)
  Pallas kernels  4.72 us (10%)
    all_gather x1, blocking collectives, per_device(): lax.all_gather(mine, 'grp', axis=0, tiled=True, axis_index_groups=halves)  18.9 us
    ppermute x1, starting transfers between devices, per_device(): cross = lax.ppermute(block, ('blk', 'grp'), cross_route)  8.26 us
    all_gather x1, blocking collectives, per_device(): lax.all_gather(block, 'grp', axis=0, tiled=True, axis_index_groups=pairs)  5.4 us
    ppermute x1, starting transfers between devices, per_device(): inside = lax.ppermute(block, ('blk', 'grp'), inside_route)  4.22 us
    all_gather x1, blocking collectives, per_device(): both = lax.all_gather(packed, 'grp', axis=0, axis_index_groups=chips)  3.14 us
    pallas_call x1, Pallas kernels, per_device(): call(last_kernel, tile, 64, GRP)  1.5 us
    pallas_call x1, Pallas kernels, per_device(): inside_tile = call(visitor_kernel, tile, 64, GRP)(row_maps, inside, weights)  1.45 us
    pallas_call x1, Pallas kernels, per_device(): own_tile, row_maps = call(own_kernel, (tile, rows), 32, 6)(block, weights)  1.03 us
  transfers between devices with their start and end apart: 2, of which 1 were waited for; matrix products, arithmetic and copies ran while one was open for 0% of the time, Pallas kernels for 5%

profile of v1, /device:TPU:1, one launch (start us, length us, event | category | flops | bytes accessed | tf_op | source)
XLA Modules:
  0.0 45.1 jit_solution(4862183505208560323)
XLA Ops:
  0.0 0.0 copy-start
  0.0 18.9 %all_gather.12 = bf16[4,48,128]{2,1,0:T(8,128)(2,1)S(1)} all-gather(bf16[1,48,128]{2,1,0:T(8,128)(2,1)} %bitcast.8), channel_id=1, replica_groups={{0,1,6,7},{2,3,4,5},{8,9,14,15},{10,11,12,13},{16,17,22,23},{18,19,20,2..., dimensions={0}, use_global_device_ids=true | all-gather | bytes 61440 | tf_op jit(solution)/shard_map/all_gather | solution.py:243
  18.9 5.4 %all_gather.13.block_ref = bf16[8,48,128]{2,1,0:T(8,128)(2,1)S(1)} all-gather(bf16[4,48,128]{2,1,0:T(8,128)(2,1)S(1)} %all_gather.12), channel_id=1, replica_groups={{0,2},{1,3},{6,4},{7,5},{8,10},{9,11},{14,12},{15,13},{16,18},{17,19},{..., dimensions={0}, use_global_device_ids=true | all-gather | bytes 147456 | tf_op jit(solution)/shard_map/all_gather | solution.py:244
  24.3 4.2 %collective-permute-start.1 = (bf16[8,48,128]{2,1,0:T(8,128)(2,1)S(1)}, bf16[8,48,128]{2,1,0:T(8,128)(2,1)S(1)}, u32[]{:S(2)}, u32[]{:S(2)}) collective-permute-start(bf16[8,48,128]{2,1,0:T(8,128)(2,1)S(1)} %all_gather.13.block_ref), channel_id=1, source_target_pairs={{17,0},{8,1},{1,8},{16,9},{9,16},{0,17},{19,2},{10,3},{3,10},{18,1... | collective-permute-start | bytes 294920 | tf_op jit(solution)/shard_map/ppermute | solution.py:246
  28.5 8.3 %collective-permute-start = (bf16[8,48,128]{2,1,0:T(8,128)(2,1)S(1)}, bf16[8,48,128]{2,1,0:T(8,128)(2,1)S(1)}, u32[]{:S(2)}, u32[]{:S(2)}) collective-permute-start(bf16[8,48,128]{2,1,0:T(8,128)(2,1)S(1)} %all_gather.13.block_ref), channel_id=1, source_target_pairs={{752,0},{760,1},{761,8},{24,9},{25,16},{32,17},{754,2},{762,3},{76... | collective-permute-start | bytes 294920 | tf_op jit(solution)/shard_map/ppermute | solution.py:247
  36.8 0.0 copy-done
  36.8 1.0 %shard_map.28 = (f32[8,128]{1,0:T(8,128)S(1)}, f32[4,9,8,128]{3,2,1,0:T(8,128)S(1)}) custom-call(bf16[8,48,128]{2,1,0:T(8,128)(2,1)S(1)} %all_gather.13.block_ref, bf16[256,256]{1,0:T(8,128)(2,1)S(1)} %copy-done), custom_call_target="tpu_custom_call" | custom-call | flops 50331648 | bytes 1048576 | tf_op jit(solution)/shard_map/pallas_call | solution.py:250
  37.8 0.0 collective-permute-done.1.block_ref
  37.9 1.4 %shard_map.29.inside_ref = f32[8,128]{1,0:T(8,128)S(1)} custom-call(f32[4,9,8,128]{3,2,1,0:T(8,128)S(1)} %get-tuple-element.7.rows_ref, bf16[8,48,128]{2,1,0:T(8,128)(2,1)S(1)} %collective-permute-done.1.block_ref, bf16[256,256]{1,0:T(8,128)(2,1)S(1)} %copy-done), custom_call_target="tpu_custom_call" | custom-call | flops 100663296 | bytes 1048576 | tf_op jit(solution)/shard_map/pallas_call | solution.py:251
  39.3 0.4 collective-permute-done.block_ref
  39.7 1.5 %shard_map.30 = f32[8,128]{1,0:T(8,128)S(1)} custom-call(f32[4,9,8,128]{3,2,1,0:T(8,128)S(1)} %get-tuple-element.7.rows_ref, bf16[8,48,128]{2,1,0:T(8,128)(2,1)S(1)} %collective-permute-done.block_ref, bf16[256,256]{1,0:T(8,128)(2,1)S(1)} %copy-done, f32[8,128]{1,0:T(8,128)S(1)} %get-tuple-element.8.own_ref, f32[8,128]{1,0:T(8,128)S(1)} %shard_map.29.inside_ref), custom_call_target="tpu_custom_call" | custom-call | flops 100663296 | bytes 1048576 | tf_op jit(solution)/shard_map/pallas_call | solution.py:252
  41.2 3.1 %all-gather = f32[16,128]{1,0:T(8,128)S(1)} all-gather(f32[8,128]{1,0:T(8,128)S(1)} %shard_map.30), channel_id=2, replica_groups={{0,1},{2,3},{4,5},{6,7},{8,9},{10,11},{12,13},{14,15},{16,17},{18,19},{..., dimensions={0}, use_global_device_ids=true | all-gather | bytes 12288 | tf_op jit(solution)/shard_map/all_gather | solution.py:254
  44.3 0.7 %shard_map.31 = f32[5,2,16]{2,1,0:T(2,128)} custom-call(f32[2,8,128]{2,1,0:T(8,128)S(1)} %bitcast.7), custom_call_target="tpu_custom_call" | custom-call | bytes 1048576 | tf_op jit(solution)/shard_map/pallas_call | solution.py:255
Async XLA Ops:
  0.0 36.8 %copy-start = (bf16[256,256]{1,0:T(8,128)(2,1)S(1)}, bf16[256,256]{1,0:T(8,128)(2,1)}, u32[]{:S(2)}) copy-start(bf16[256,256]{1,0:T(8,128)(2,1)} %constant.2.clone.weights_ref) | copy-start | bytes 393220
  24.3 13.5 %collective-permute-start.1 = (bf16[8,48,128]{2,1,0:T(8,128)(2,1)S(1)}, bf16[8,48,128]{2,1,0:T(8,128)(2,1)S(1)}, u32[]{:S(2)}, u32[]{:S(2)}) collective-permute-start(bf16[8,48,128]{2,1,0:T(8,128)(2,1)S(1)} %all_gather.13.block_ref), channel_id=1, source_target_pairs={{17,0},{8,1},{1,8},{16,9},{9,16},{0,17},{19,2},{10,3},{3,10},{18,1... | collective-permute-start | bytes 294920 | tf_op jit(solution)/shard_map/ppermute | solution.py:246
  28.5 11.2 %collective-permute-start = (bf16[8,48,128]{2,1,0:T(8,128)(2,1)S(1)}, bf16[8,48,128]{2,1,0:T(8,128)(2,1)S(1)}, u32[]{:S(2)}, u32[]{:S(2)}) collective-permute-start(bf16[8,48,128]{2,1,0:T(8,128)(2,1)S(1)} %all_gather.13.block_ref), channel_id=1, source_target_pairs={{752,0},{760,1},{761,8},{24,9},{25,16},{32,17},{754,2},{762,3},{76... | collective-permute-start | bytes 294920 | tf_op jit(solution)/shard_map/ppermute | solution.py:247

commit v2 on v1

--- a/solution.py
+++ b/solution.py
@@ -13,6 +13,8 @@
 CHIP_ROWS = 4
 GRP = 8
 bias_var = 0.1
+
+ORDER = (0, 2, 4, 6, 5, 7, 1, 3)
 
 TAIL = (
     0.3001054023535799,
@@ -153,10 +155,10 @@
 def own_kernel(block_ref, weights_ref, tile_ref, rows_ref, spread):
     place = lax.axis_index("grp")
     chip, core = place // 2, place % 2
-    at = 2 * jnp.where(chip == 0, 0, jnp.where(chip == 1, 2, jnp.where(chip == 2, 3, 1)))
-    rows = load_images(block_ref, (at, at + 1), spread)
-    first, second = jnp.where(core == 0, 0, 6), jnp.where(core == 0, 4, 2)
-    columns = load_images(block_ref, (first, first + 1, second, second + 1), spread, 2)
+    at = jnp.where(chip == 0, 0, jnp.where(chip == 1, 4, jnp.where(chip == 2, 5, 1)))
+    rows = load_images(block_ref, (at, at + 2), spread)
+    half = [jnp.where(core == 0, ORDER[n], ORDER[n + 4]) for n in range(4)]
+    columns = load_images(block_ref, half, spread, 2)
     tile, row_maps = pair_tile(rows, columns, weights_ref[...])
     tile_ref[...] = tile
     rows_ref[:, :3] = rows
@@ -166,7 +168,7 @@
 
 
 def visitor_tile(rows_ref, block_ref, weights_ref, spread):
-    columns = load_images(block_ref, (0, 1, 4, 5, 6, 7, 2, 3), spread)
+    columns = load_images(block_ref, ORDER, spread)
     row_maps = [(rows_ref[:, 3 + layer], rows_ref[:, 6 + layer]) for layer in range(LAYERS)]
     return pair_tile(rows_ref[:, :3], columns, weights_ref[...], row_maps)[0]
 
@@ -186,11 +188,11 @@
     low, high = [jnp.where(core == 0, both_ref[at, :2], both_ref[at, 2:4]) for at in (0, 1)]
     low_inside, high_inside = low[:, 8:24], high[:, 8:24]
     low_cross, high_cross = low[:, 24:40], high[:, 24:40]
-    out_ref[0] = jnp.where(level == 2, high_inside, low_cross)
-    out_ref[1] = jnp.where(level == 0, high_cross, low_inside)
+    out_ref[0] = jnp.where(level == 2, low_inside, low_cross)
+    out_ref[1] = jnp.where(level == 0, high_cross, high_inside)
     out_ref[2] = jnp.concatenate([low[:, :8], high[:, :8]], 1)
-    out_ref[3] = jnp.where(level == 2, low_cross, high_inside)
-    out_ref[4] = jnp.where(level == 0, low_inside, high_cross)
+    out_ref[3] = jnp.where(level == 2, low_cross, low_inside)
+    out_ref[4] = jnp.where(level == 0, high_inside, high_cross)
 
 
 def call(body, outs, pairs, places):
@@ -230,7 +232,7 @@
                     turn = used.get(sender, 0)
                     used[sender] = turn + 1
                     cross.append((device(*sender, turn), here))
-                    source = (level + (1 if core else 2)) % 3
+                    source = (level + (2 if core else 1)) % 3
                     inside.append((device(line, source, chip, 1 - core), here))
     return cross, inside
 
@@ -238,10 +240,10 @@
 def per_device(images):
     weights = jnp.asarray(stencil_weights(), jnp.bfloat16)
     mine = images.reshape(2, 3, 8, 128).transpose(1, 2, 0, 3).reshape(1, 48, 128)
-    halves = [[0, 1, 6, 7], [2, 3, 4, 5]]
-    pairs = [[0, 2], [1, 3], [6, 4], [7, 5]]
-    block = lax.all_gather(mine, "grp", axis=0, tiled=True, axis_index_groups=halves)
-    block = lax.all_gather(block, "grp", axis=0, tiled=True, axis_index_groups=pairs)
+    pairs = [[0, 6], [1, 7], [2, 4], [3, 5]]
+    halves = [[0, 1, 2, 3], [6, 7, 4, 5]]
+    block = lax.all_gather(mine, "grp", axis=0, tiled=True, axis_index_groups=pairs)
+    block = lax.all_gather(block, "grp", axis=0, tiled=True, axis_index_groups=halves)
     cross_route, inside_route = routes()
     inside = lax.ppermute(block, ("blk", "grp"), inside_route)
     cross = lax.ppermute(block, ("blk", "grp"), cross_route)

time: 45.2 us -> 44.5 us (0.985)
  starting transfers between devices: 12.5 us -> 11 us
  waiting for transfers between devices: 0.39 us -> 1.41 us
    all_gather x1, blocking collectives: 3.14 us -> 1.79 us  [per_device(): both = lax.all_gather(packed, 'grp', axis=0, axis_index_groups=chips)]
    ppermute x1, starting transfers between devices: 8.26 us -> 7.14 us  [per_device(): cross = lax.ppermute(block, ('blk', 'grp'), cross_route)]
    all_gather x2, blocking collectives: 24.3 us -> 25.4 us  [the longest x1 15.4 us: per_device(): lax.all_gather(mine, 'grp', axis=0, tiled=True, axis_index_groups=pairs)]
    ppermute x1, waiting for transfers between devices: 0.39 us -> 1.41 us  [per_device(): cross = lax.ppermute(block, ('blk', 'grp'), cross_route)]
  transfers between devices with their start and end apart: 2 -> 2, of which waited for: 1 -> 1; matrix products, arithmetic and copies ran while one was open for 0% -> 0% of each run, Pallas kernels for 5% -> 6%
where the time goes in v2:
time: 44.5 us; the launch traced here: 44.3 us
  blocking collectives  27.2 us (61%)
  starting transfers between devices  11 us (25%)
  Pallas kernels  4.72 us (11%)
  waiting for transfers between devices  1.41 us (3%)
    all_gather x1, blocking collectives, per_device(): lax.all_gather(mine, 'grp', axis=0, tiled=True, axis_index_groups=pairs)  15.4 us
    all_gather x1, blocking collectives, per_device(): lax.all_gather(block, 'grp', axis=0, tiled=True, axis_index_groups=halves)  10 us
    ppermute x1, starting transfers between devices, per_device(): cross = lax.ppermute(block, ('blk', 'grp'), cross_route)  7.14 us
    ppermute x1, starting transfers between devices, per_device(): inside = lax.ppermute(block, ('blk', 'grp'), inside_route)  3.85 us
    all_gather x1, blocking collectives, per_device(): both = lax.all_gather(packed, 'grp', axis=0, axis_index_groups=chips)  1.79 us
    pallas_call x1, Pallas kernels, per_device(): call(last_kernel, tile, 64, GRP)  1.5 us
    pallas_call x1, Pallas kernels, per_device(): inside_tile = call(visitor_kernel, tile, 64, GRP)(row_maps, inside, weights)  1.45 us
    ppermute x1, waiting for transfers between devices, per_device(): cross = lax.ppermute(block, ('blk', 'grp'), cross_route)  1.41 us
  transfers between devices with their start and end apart: 2, of which 1 were waited for; matrix products, arithmetic and copies ran while one was open for 0% of the time, Pallas kernels for 6%

profile of v2, /device:TPU:1, one launch (start us, length us, event | category | flops | bytes accessed | tf_op | source)
XLA Modules:
  0.0 44.3 jit_solution(8571224307133671073)
XLA Ops:
  0.0 0.0 copy-start
  0.0 15.4 %all_gather.12 = bf16[2,48,128]{2,1,0:T(8,128)(2,1)S(1)} all-gather(bf16[1,48,128]{2,1,0:T(8,128)(2,1)} %bitcast.8), channel_id=1, replica_groups={{0,6},{1,7},{2,4},{3,5},{8,14},{9,15},{10,12},{11,13},{16,22},{17,23},{..., dimensions={0}, use_global_device_ids=true | all-gather | bytes 36864 | tf_op jit(solution)/shard_map/all_gather | solution.py:245
  15.4 10.0 %all_gather.13.block_ref = bf16[8,48,128]{2,1,0:T(8,128)(2,1)S(1)} all-gather(bf16[2,48,128]{2,1,0:T(8,128)(2,1)S(1)} %all_gather.12), channel_id=1, replica_groups={{0,1,2,3},{6,7,4,5},{8,9,10,11},{14,15,12,13},{16,17,18,19},{22,23,20,2..., dimensions={0}, use_global_device_ids=true | all-gather | bytes 122880 | tf_op jit(solution)/shard_map/all_gather | solution.py:246
  25.4 3.9 %collective-permute-start.1 = (bf16[8,48,128]{2,1,0:T(8,128)(2,1)S(1)}, bf16[8,48,128]{2,1,0:T(8,128)(2,1)S(1)}, u32[]{:S(2)}, u32[]{:S(2)}) collective-permute-start(bf16[8,48,128]{2,1,0:T(8,128)(2,1)S(1)} %all_gather.13.block_ref), channel_id=1, source_target_pairs={{9,0},{16,1},{17,8},{0,9},{1,16},{8,17},{11,2},{18,3},{19,10},{2,1... | collective-permute-start | bytes 294920 | tf_op jit(solution)/shard_map/ppermute | solution.py:248
  29.3 7.1 %collective-permute-start = (bf16[8,48,128]{2,1,0:T(8,128)(2,1)S(1)}, bf16[8,48,128]{2,1,0:T(8,128)(2,1)S(1)}, u32[]{:S(2)}, u32[]{:S(2)}) collective-permute-start(bf16[8,48,128]{2,1,0:T(8,128)(2,1)S(1)} %all_gather.13.block_ref), channel_id=1, source_target_pairs={{752,0},{760,1},{761,8},{24,9},{25,16},{32,17},{754,2},{762,3},{76... | collective-permute-start | bytes 294920 | tf_op jit(solution)/shard_map/ppermute | solution.py:249
  36.4 0.0 copy-done
  36.4 1.0 %shard_map.28 = (f32[8,128]{1,0:T(8,128)S(1)}, f32[4,9,8,128]{3,2,1,0:T(8,128)S(1)}) custom-call(bf16[8,48,128]{2,1,0:T(8,128)(2,1)S(1)} %all_gather.13.block_ref, bf16[256,256]{1,0:T(8,128)(2,1)S(1)} %copy-done), custom_call_target="tpu_custom_call" | custom-call | flops 50331648 | bytes 1048576 | tf_op jit(solution)/shard_map/pallas_call | solution.py:252
  37.5 0.0 collective-permute-done.1.block_ref
  37.5 1.4 %shard_map.29.inside_ref = f32[8,128]{1,0:T(8,128)S(1)} custom-call(f32[4,9,8,128]{3,2,1,0:T(8,128)S(1)} %get-tuple-element.7.rows_ref, bf16[8,48,128]{2,1,0:T(8,128)(2,1)S(1)} %collective-permute-done.1.block_ref, bf16[256,256]{1,0:T(8,128)(2,1)S(1)} %copy-done), custom_call_target="tpu_custom_call" | custom-call | flops 100663296 | bytes 1048576 | tf_op jit(solution)/shard_map/pallas_call | solution.py:253
  38.9 1.4 %collective-permute-done.block_ref = bf16[8,48,128]{2,1,0:T(8,128)(2,1)S(1)} collective-permute-done((bf16[8,48,128]{2,1,0:T(8,128)(2,1)S(1)}, bf16[8,48,128]{2,1,0:T(8,128)(2,1)S(1)}, u32[]{:S(2)}, u32[]{:S(2)}) %collective-permute-start) | collective-permute-done | bytes 98336 | tf_op jit(solution)/shard_map/ppermute | solution.py:249
  40.3 1.5 %shard_map.30 = f32[8,128]{1,0:T(8,128)S(1)} custom-call(f32[4,9,8,128]{3,2,1,0:T(8,128)S(1)} %get-tuple-element.7.rows_ref, bf16[8,48,128]{2,1,0:T(8,128)(2,1)S(1)} %collective-permute-done.block_ref, bf16[256,256]{1,0:T(8,128)(2,1)S(1)} %copy-done, f32[8,128]{1,0:T(8,128)S(1)} %get-tuple-element.8.own_ref, f32[8,128]{1,0:T(8,128)S(1)} %shard_map.29.inside_ref), custom_call_target="tpu_custom_call" | custom-call | flops 100663296 | bytes 1048576 | tf_op jit(solution)/shard_map/pallas_call | solution.py:254
  41.8 1.8 %all-gather = f32[16,128]{1,0:T(8,128)S(1)} all-gather(f32[8,128]{1,0:T(8,128)S(1)} %shard_map.30), channel_id=2, replica_groups={{0,1},{2,3},{4,5},{6,7},{8,9},{10,11},{12,13},{14,15},{16,17},{18,19},{..., dimensions={0}, use_global_device_ids=true | all-gather | bytes 12288 | tf_op jit(solution)/shard_map/all_gather | solution.py:256
  43.6 0.7 %shard_map.31 = f32[5,2,16]{2,1,0:T(2,128)} custom-call(f32[2,8,128]{2,1,0:T(8,128)S(1)} %bitcast.7), custom_call_target="tpu_custom_call" | custom-call | bytes 1048576 | tf_op jit(solution)/shard_map/pallas_call | solution.py:257
Async XLA Ops:
  0.0 36.4 %copy-start = (bf16[256,256]{1,0:T(8,128)(2,1)S(1)}, bf16[256,256]{1,0:T(8,128)(2,1)}, u32[]{:S(2)}) copy-start(bf16[256,256]{1,0:T(8,128)(2,1)} %constant.2.clone.weights_ref) | copy-start | bytes 393220
  25.4 12.1 %collective-permute-start.1 = (bf16[8,48,128]{2,1,0:T(8,128)(2,1)S(1)}, bf16[8,48,128]{2,1,0:T(8,128)(2,1)S(1)}, u32[]{:S(2)}, u32[]{:S(2)}) collective-permute-start(bf16[8,48,128]{2,1,0:T(8,128)(2,1)S(1)} %all_gather.13.block_ref), channel_id=1, source_target_pairs={{9,0},{16,1},{17,8},{0,9},{1,16},{8,17},{11,2},{18,3},{19,10},{2,1... | collective-permute-start | bytes 294920 | tf_op jit(solution)/shard_map/ppermute | solution.py:248
  29.3 11.1 %collective-permute-start = (bf16[8,48,128]{2,1,0:T(8,128)(2,1)S(1)}, bf16[8,48,128]{2,1,0:T(8,128)(2,1)S(1)}, u32[]{:S(2)}, u32[]{:S(2)}) collective-permute-start(bf16[8,48,128]{2,1,0:T(8,128)(2,1)S(1)} %all_gather.13.block_ref), channel_id=1, source_target_pairs={{752,0},{760,1},{761,8},{24,9},{25,16},{32,17},{754,2},{762,3},{76... | collective-permute-start | bytes 294920 | tf_op jit(solution)/shard_map/ppermute | solution.py:249

commit v3 on v2

--- a/solution.py
+++ b/solution.py
@@ -98,16 +98,6 @@
     return maps[0]
 
 
-def lane_sums(rows):
-    ones = jnp.ones((8, 256), jnp.bfloat16)
-    return lax.dot_general(
-        ones,
-        jnp.concatenate(split(rows), 1),
-        (((1,), (1,)), ((), ())),
-        preferred_element_type=jnp.float32,
-    )
-
-
 def squares(channels):
     return jnp.sum(channels * channels, 1) * (1.0 / 27.0)
 
@@ -116,17 +106,17 @@
     above, below = masks()
     count = columns.shape[0]
     pairs = CHIP_ROWS * count
-    products = []
+    maps = []
     for row in range(CHIP_ROWS):
         terms = (row_channels[row] * (1.0 / 27.0))[None] * columns
-        products.append(terms[:, 0] + terms[:, 1] + terms[:, 2])
-    maps = products + [squares(columns)]
+        maps.append(terms[:, 0] + terms[:, 1] + terms[:, 2])
+    squared = squares(columns)
     if row_maps is None:
-        maps.append(squares(row_channels))
+        squared = jnp.concatenate([squared, squares(row_channels)], 0)
     made = []
     for layer in range(LAYERS):
+        variance = stencil_sum(squared, weights, above, below) + bias_var
         sums = stencil_sum(jnp.concatenate(maps, 0), weights, above, below) + bias_var
-        variance = sums[pairs:]
         inverse = lax.rsqrt(variance)
         scale = variance * inverse
         if row_maps is None:
@@ -140,15 +130,18 @@
             part = sums[row * count : (row + 1) * count]
             ratio = part * (row_inverse[row][None] * inverse[:count])
             maps.append((row_scale[row][None] * scale[:count]) * relu_over_scale(ratio))
-        if layer < LAYERS - 1:
-            maps.append(variance * (1.0 / 9.0))
-    tile = jnp.zeros((8, 128), jnp.float32)
+        squared = variance * (1.0 / 9.0)
     sub = lax.broadcasted_iota(jnp.int32, (8, 128), 0)
+    lane = lax.broadcasted_iota(jnp.int32, (8, 128), 1)
+    spots = []
     for row in range(CHIP_ROWS):
-        folded = [fold(maps[row][group : group + 8]) for group in range(0, count, 8)]
-        sums = lane_sums(jnp.concatenate(folded, 0))
-        sums = jnp.concatenate([sums, jnp.zeros((8, 128 - count), jnp.float32)], 1)
-        tile = jnp.where(sub == row, sums, tile)
+        spot = jnp.zeros((8, 128), jnp.float32)
+        for group in range(0, count, 8):
+            total = jnp.sum(fold(maps[row][group : group + 8]), 1, keepdims=True)
+            spot = jnp.where(lane == sub + group, total, spot)
+        spots.append(spot)
+    spots += [jnp.zeros((8, 128), jnp.float32)] * (8 - CHIP_ROWS)
+    tile = fold(jnp.stack(spots, 0))
     return tile, made
 
 
@@ -177,22 +170,19 @@
     tile_ref[...] = visitor_tile(rows_ref, block_ref, weights_ref, spread)
 
 
-def last_kernel(rows_ref, block_ref, weights_ref, own_ref, inside_ref, tile_ref, spread):
-    cross = visitor_tile(rows_ref, block_ref, weights_ref, spread)
-    tile_ref[...] = own_ref[...] + pltpu.roll(inside_ref[...], 8, 1) + pltpu.roll(cross, 24, 1)
+def last_kernel(rows_ref, block_ref, weights_ref, own_ref, before_ref, tile_ref, spread):
+    after = visitor_tile(rows_ref, block_ref, weights_ref, spread)
+    tile_ref[...] = own_ref[...] + pltpu.roll(before_ref[...], 8, 1) + pltpu.roll(after, 24, 1)
 
 
 def assemble_kernel(both_ref, out_ref):
-    level = lax.axis_index("blk") % 3
     core = lax.axis_index("grp") % 2
     low, high = [jnp.where(core == 0, both_ref[at, :2], both_ref[at, 2:4]) for at in (0, 1)]
-    low_inside, high_inside = low[:, 8:24], high[:, 8:24]
-    low_cross, high_cross = low[:, 24:40], high[:, 24:40]
-    out_ref[0] = jnp.where(level == 2, low_inside, low_cross)
-    out_ref[1] = jnp.where(level == 0, high_cross, high_inside)
+    out_ref[0] = high[:, 8:24]
+    out_ref[1] = low[:, 8:24]
     out_ref[2] = jnp.concatenate([low[:, :8], high[:, :8]], 1)
-    out_ref[3] = jnp.where(level == 2, low_cross, low_inside)
-    out_ref[4] = jnp.where(level == 0, high_inside, high_cross)
+    out_ref[3] = low[:, 24:40]
+    out_ref[4] = high[:, 24:40]
 
 
 def call(body, outs, pairs, places):
@@ -207,34 +197,13 @@
     )
 
 
-def routes():
-    lines = 32
-
-    def device(line, level, chip, core):
-        return ((line % lines) * 3 + level) * GRP + chip * 2 + core
-
-    across = {
-        (0, 0): (-1, 1),
-        (0, 1): (-1, 2),
-        (1, 0): (-1, 2),
-        (1, 1): (1, 0),
-        (2, 0): (1, 0),
-        (2, 1): (1, 1),
-    }
-    cross, inside, used = [], [], {}
-    for line in range(lines):
-        for chip in range(GRP // 2):
-            for level in range(3):
-                for core in (0, 1):
-                    here = device(line, level, chip, core)
-                    step, source = across[level, core]
-                    sender = (line + step) % lines, source, chip
-                    turn = used.get(sender, 0)
-                    used[sender] = turn + 1
-                    cross.append((device(*sender, turn), here))
-                    source = (level + (2 if core else 1)) % 3
-                    inside.append((device(line, source, chip, 1 - core), here))
-    return cross, inside
+def by_core(block, direction, blocks):
+    route = []
+    for block_index in range(blocks):
+        for place in range(GRP):
+            source = (block_index + direction * (place % 2 + 1)) % blocks
+            route.append((source * GRP + place, block_index * GRP + place))
+    return lax.ppermute(block, ("blk", "grp"), route)
 
 
 def per_device(images):
@@ -244,14 +213,14 @@
     halves = [[0, 1, 2, 3], [6, 7, 4, 5]]
     block = lax.all_gather(mine, "grp", axis=0, tiled=True, axis_index_groups=pairs)
     block = lax.all_gather(block, "grp", axis=0, tiled=True, axis_index_groups=halves)
-    cross_route, inside_route = routes()
-    inside = lax.ppermute(block, ("blk", "grp"), inside_route)
-    cross = lax.ppermute(block, ("blk", "grp"), cross_route)
+    blocks = lax.axis_size("blk")
+    before = by_core(block, -1, blocks)
+    after = by_core(block, 1, blocks)
     tile = jax.ShapeDtypeStruct((8, 128), jnp.float32)
     rows = jax.ShapeDtypeStruct((CHIP_ROWS, 9, 8, 128), jnp.float32)
     own_tile, row_maps = call(own_kernel, (tile, rows), 32, 6)(block, weights)
-    inside_tile = call(visitor_kernel, tile, 64, GRP)(row_maps, inside, weights)
-    packed = call(last_kernel, tile, 64, GRP)(row_maps, cross, weights, own_tile, inside_tile)
+    before_tile = call(visitor_kernel, tile, 64, GRP)(row_maps, before, weights)
+    packed = call(last_kernel, tile, 64, GRP)(row_maps, after, weights, own_tile, before_tile)
     chips = [[2 * chip, 2 * chip + 1] for chip in range(GRP // 2)]
     both = lax.all_gather(packed, "grp", axis=0, axis_index_groups=chips)
     result = call(assemble_kernel, jax.ShapeDtypeStruct((5, 2, 16), jnp.float32), 0, 0)(both)

time: 44.5 us -> 43 us (0.966)
  blocking collectives: 27.2 us -> 28.9 us
  waiting for transfers between devices: 1.41 us -> 0.01 us
  starting transfers between devices: 11 us -> 9.91 us
  Pallas kernels: 4.72 us -> 3.93 us
    all_gather x1, blocking collectives: 1.79 us -> 3.53 us  [per_device(): both = lax.all_gather(packed, 'grp', axis=0, axis_index_groups=chips)]
    ppermute x2, waiting for transfers between devices: 1.41 us -> 0.01 us  [by_core(): return lax.ppermute(block, ('blk', 'grp'), route)]
    ppermute x2, starting transfers between devices: 11 us -> 9.91 us  [by_core(): return lax.ppermute(block, ('blk', 'grp'), route)]
  transfers between devices with their start and end apart: 2 -> 2, of which waited for: 1 -> 0; matrix products, arithmetic and copies ran while one was open for 0% -> 0% of each run, Pallas kernels for 6% -> 5%
where the time goes in v3:
time: 43 us; the launch traced here: 42.8 us
  blocking collectives  28.9 us (67%)
  starting transfers between devices  9.91 us (23%)
  Pallas kernels  3.93 us (9%)
    all_gather x1, blocking collectives, per_device(): lax.all_gather(mine, 'grp', axis=0, tiled=True, axis_index_groups=pairs)  15.4 us
    all_gather x1, blocking collectives, per_device(): lax.all_gather(block, 'grp', axis=0, tiled=True, axis_index_groups=halves)  10 us
    ppermute x2, starting transfers between devices, by_core(): return lax.ppermute(block, ('blk', 'grp'), route)  9.91 us
    all_gather x1, blocking collectives, per_device(): both = lax.all_gather(packed, 'grp', axis=0, axis_index_groups=chips)  3.53 us
    pallas_call x1, Pallas kernels, per_device(): call(last_kernel, tile, 64, GRP)  1.28 us
    pallas_call x1, Pallas kernels, per_device(): before_tile = call(visitor_kernel, tile, 64, GRP)(row_maps, before, weights)  1.22 us
  transfers between devices with their start and end apart: 2, of which 0 were waited for; matrix products, arithmetic and copies ran while one was open for 0% of the time, Pallas kernels for 5%

profile of v3, /device:TPU:1, one launch (start us, length us, event | category | flops | bytes accessed | tf_op | source)
XLA Modules:
  0.0 42.8 jit_solution(3709780853908844600)
XLA Ops:
  0.0 0.0 copy-start
  0.0 15.4 %all_gather.12 = bf16[2,48,128]{2,1,0:T(8,128)(2,1)S(1)} all-gather(bf16[1,48,128]{2,1,0:T(8,128)(2,1)} %bitcast.8), channel_id=1, replica_groups={{0,6},{1,7},{2,4},{3,5},{8,14},{9,15},{10,12},{11,13},{16,22},{17,23},{..., dimensions={0}, use_global_device_ids=true | all-gather | bytes 36864 | tf_op jit(solution)/shard_map/all_gather | solution.py:214
  15.4 10.0 %all_gather.13.block_ref = bf16[8,48,128]{2,1,0:T(8,128)(2,1)S(1)} all-gather(bf16[2,48,128]{2,1,0:T(8,128)(2,1)S(1)} %all_gather.12), channel_id=1, replica_groups={{0,1,2,3},{6,7,4,5},{8,9,10,11},{14,15,12,13},{16,17,18,19},{22,23,20,2..., dimensions={0}, use_global_device_ids=true | all-gather | bytes 122880 | tf_op jit(solution)/shard_map/all_gather | solution.py:215
  25.4 3.8 %collective-permute-start.1 = (bf16[8,48,128]{2,1,0:T(8,128)(2,1)S(1)}, bf16[8,48,128]{2,1,0:T(8,128)(2,1)S(1)}, u32[]{:S(2)}, u32[]{:S(2)}) collective-permute-start(bf16[8,48,128]{2,1,0:T(8,128)(2,1)S(1)} %all_gather.13.block_ref), channel_id=1, source_target_pairs={{760,0},{753,1},{762,2},{755,3},{764,4},{757,5},{766,6},{759,7},{0... | collective-permute-start | bytes 294920 | tf_op jit(solution)/shard_map/ppermute | solution.py:206
  29.2 6.1 %collective-permute-start = (bf16[8,48,128]{2,1,0:T(8,128)(2,1)S(1)}, bf16[8,48,128]{2,1,0:T(8,128)(2,1)S(1)}, u32[]{:S(2)}, u32[]{:S(2)}) collective-permute-start(bf16[8,48,128]{2,1,0:T(8,128)(2,1)S(1)} %all_gather.13.block_ref), channel_id=1, source_target_pairs={{8,0},{17,1},{10,2},{19,3},{12,4},{21,5},{14,6},{23,7},{16,8},{25,... | collective-permute-start | bytes 294920 | tf_op jit(solution)/shard_map/ppermute | solution.py:206
  35.3 0.0 copy-done
  35.3 0.8 %shard_map.28 = (f32[8,128]{1,0:T(8,128)S(1)}, f32[4,9,8,128]{3,2,1,0:T(8,128)S(1)}) custom-call(bf16[8,48,128]{2,1,0:T(8,128)(2,1)S(1)} %all_gather.13.block_ref, bf16[256,256]{1,0:T(8,128)(2,1)S(1)} %copy-done), custom_call_target="tpu_custom_call" | custom-call | flops 50331648 | bytes 1048576 | tf_op jit(solution)/shard_map/pallas_call | solution.py:221
  36.1 0.0 collective-permute-done.1.block_ref
  36.1 1.2 %shard_map.29.before_ref = f32[8,128]{1,0:T(8,128)S(1)} custom-call(f32[4,9,8,128]{3,2,1,0:T(8,128)S(1)} %get-tuple-element.7.rows_ref, bf16[8,48,128]{2,1,0:T(8,128)(2,1)S(1)} %collective-permute-done.1.block_ref, bf16[256,256]{1,0:T(8,128)(2,1)S(1)} %copy-done), custom_call_target="tpu_custom_call" | custom-call | flops 100663296 | bytes 1048576 | tf_op jit(solution)/shard_map/pallas_call | solution.py:222
  37.3 0.0 collective-permute-done.block_ref
  37.3 1.3 %shard_map.30 = f32[8,128]{1,0:T(8,128)S(1)} custom-call(f32[4,9,8,128]{3,2,1,0:T(8,128)S(1)} %get-tuple-element.7.rows_ref, bf16[8,48,128]{2,1,0:T(8,128)(2,1)S(1)} %collective-permute-done.block_ref, bf16[256,256]{1,0:T(8,128)(2,1)S(1)} %copy-done, f32[8,128]{1,0:T(8,128)S(1)} %get-tuple-element.8.own_ref, f32[8,128]{1,0:T(8,128)S(1)} %shard_map.29.before_ref), custom_call_target="tpu_custom_call" | custom-call | flops 100663296 | bytes 1048576 | tf_op jit(solution)/shard_map/pallas_call | solution.py:223
  38.6 3.5 %all-gather = f32[16,128]{1,0:T(8,128)S(1)} all-gather(f32[8,128]{1,0:T(8,128)S(1)} %shard_map.30), channel_id=2, replica_groups={{0,1},{2,3},{4,5},{6,7},{8,9},{10,11},{12,13},{14,15},{16,17},{18,19},{..., dimensions={0}, use_global_device_ids=true | all-gather | bytes 12288 | tf_op jit(solution)/shard_map/all_gather | solution.py:225
  42.1 0.7 %shard_map.31 = f32[5,2,16]{2,1,0:T(2,128)} custom-call(f32[2,8,128]{2,1,0:T(8,128)S(1)} %bitcast.7), custom_call_target="tpu_custom_call" | custom-call | bytes 1048576 | tf_op jit(solution)/shard_map/pallas_call | solution.py:226
Async XLA Ops:
  0.0 35.3 %copy-start = (bf16[256,256]{1,0:T(8,128)(2,1)S(1)}, bf16[256,256]{1,0:T(8,128)(2,1)}, u32[]{:S(2)}) copy-start(bf16[256,256]{1,0:T(8,128)(2,1)} %constant.2.clone.weights_ref) | copy-start | bytes 393220
  25.4 10.7 %collective-permute-start.1 = (bf16[8,48,128]{2,1,0:T(8,128)(2,1)S(1)}, bf16[8,48,128]{2,1,0:T(8,128)(2,1)S(1)}, u32[]{:S(2)}, u32[]{:S(2)}) collective-permute-start(bf16[8,48,128]{2,1,0:T(8,128)(2,1)S(1)} %all_gather.13.block_ref), channel_id=1, source_target_pairs={{760,0},{753,1},{762,2},{755,3},{764,4},{757,5},{766,6},{759,7},{0... | collective-permute-start | bytes 294920 | tf_op jit(solution)/shard_map/ppermute | solution.py:206
  29.2 8.1 %collective-permute-start = (bf16[8,48,128]{2,1,0:T(8,128)(2,1)S(1)}, bf16[8,48,128]{2,1,0:T(8,128)(2,1)S(1)}, u32[]{:S(2)}, u32[]{:S(2)}) collective-permute-start(bf16[8,48,128]{2,1,0:T(8,128)(2,1)S(1)} %all_gather.13.block_ref), channel_id=1, source_target_pairs={{8,0},{17,1},{10,2},{19,3},{12,4},{21,5},{14,6},{23,7},{16,8},{25,... | collective-permute-start | bytes 294920 | tf_op jit(solution)/shard_map/ppermute | solution.py:206

commit v4 on v3

--- a/solution.py
+++ b/solution.py
@@ -77,11 +77,11 @@
 
 
 def relu_over_scale(ratio):
-    gap = 1.0 - jnp.minimum(jnp.abs(ratio), 1.0)
+    gap = jnp.maximum(1.0 - jnp.abs(ratio), 1e-30)
     poly = jnp.float32(TAIL[-1])
     for coefficient in TAIL[-2::-1]:
         poly = poly * gap + jnp.float32(coefficient)
-    return jnp.clip(ratio, 0.0, 1.0) + gap * gap * lax.rsqrt(jnp.maximum(gap, 1e-30)) * poly
+    return jnp.clip(ratio, 0.0, 1.0) + gap * gap * lax.rsqrt(gap) * poly
 
 
 def fold(maps):
@@ -116,7 +116,6 @@
     made = []
     for layer in range(LAYERS):
         variance = stencil_sum(squared, weights, above, below) + bias_var
-        sums = stencil_sum(jnp.concatenate(maps, 0), weights, above, below) + bias_var
         inverse = lax.rsqrt(variance)
         scale = variance * inverse
         if row_maps is None:
@@ -125,11 +124,10 @@
             made.append((row_inverse, row_scale))
         else:
             row_inverse, row_scale = row_maps[layer]
-        maps = []
         for row in range(CHIP_ROWS):
-            part = sums[row * count : (row + 1) * count]
-            ratio = part * (row_inverse[row][None] * inverse[:count])
-            maps.append((row_scale[row][None] * scale[:count]) * relu_over_scale(ratio))
+            cov = stencil_sum(maps[row], weights, above, below) + bias_var
+            ratio = cov * (row_inverse[row][None] * inverse[:count])
+            maps[row] = (row_scale[row][None] * scale[:count]) * relu_over_scale(ratio)
         squared = variance * (1.0 / 9.0)
     sub = lax.broadcasted_iota(jnp.int32, (8, 128), 0)
     lane = lax.broadcasted_iota(jnp.int32, (8, 128), 1)
@@ -178,11 +176,11 @@
 def assemble_kernel(both_ref, out_ref):
     core = lax.axis_index("grp") % 2
     low, high = [jnp.where(core == 0, both_ref[at, :2], both_ref[at, 2:4]) for at in (0, 1)]
-    out_ref[0] = high[:, 8:24]
-    out_ref[1] = low[:, 8:24]
+    out_ref[0] = low[:, 8:24]
+    out_ref[1] = high[:, 8:24]
     out_ref[2] = jnp.concatenate([low[:, :8], high[:, :8]], 1)
-    out_ref[3] = low[:, 24:40]
-    out_ref[4] = high[:, 24:40]
+    out_ref[3] = high[:, 24:40]
+    out_ref[4] = low[:, 24:40]
 
 
 def call(body, outs, pairs, places):
@@ -197,11 +195,12 @@
     )
 
 
-def by_core(block, direction, blocks):
+def by_core(block, direction, nearer, blocks):
     route = []
     for block_index in range(blocks):
         for place in range(GRP):
-            source = (block_index + direction * (place % 2 + 1)) % blocks
+            step = place % 2 + 1 if nearer else 2 - place % 2
+            source = (block_index + direction * step) % blocks
             route.append((source * GRP + place, block_index * GRP + place))
     return lax.ppermute(block, ("blk", "grp"), route)
 
@@ -214,8 +213,8 @@
     block = lax.all_gather(mine, "grp", axis=0, tiled=True, axis_index_groups=pairs)
     block = lax.all_gather(block, "grp", axis=0, tiled=True, axis_index_groups=halves)
     blocks = lax.axis_size("blk")
-    before = by_core(block, -1, blocks)
-    after = by_core(block, 1, blocks)
+    before = by_core(block, -1, False, blocks)
+    after = by_core(block, 1, False, blocks)
     tile = jax.ShapeDtypeStruct((8, 128), jnp.float32)
     rows = jax.ShapeDtypeStruct((CHIP_ROWS, 9, 8, 128), jnp.float32)
     own_tile, row_maps = call(own_kernel, (tile, rows), 32, 6)(block, weights)

time: 43 us -> 42.4 us (0.986)
  blocking collectives: 28.9 us -> 27.2 us
  starting transfers between devices: 9.91 us -> 10.9 us
    all_gather x1, blocking collectives: 3.53 us -> 1.79 us  [per_device(): both = lax.all_gather(packed, 'grp', axis=0, axis_index_groups=chips)]
    ppermute x2, starting transfers between devices: 9.91 us -> 10.9 us  [by_core(): return lax.ppermute(block, ('blk', 'grp'), route)]
  transfers between devices with their start and end apart: 2 -> 2, of which waited for: 0 -> 2; matrix products, arithmetic and copies ran while one was open for 0% -> 0% of each run, Pallas kernels for 5% -> 5%
where the time goes in v4:
time: 42.4 us; the launch traced here: 42.2 us
  blocking collectives  27.2 us (64%)
  starting transfers between devices  10.9 us (26%)
  Pallas kernels  3.86 us (9%)
    all_gather x1, blocking collectives, per_device(): lax.all_gather(mine, 'grp', axis=0, tiled=True, axis_index_groups=pairs)  15.4 us
    ppermute x2, starting transfers between devices, by_core(): return lax.ppermute(block, ('blk', 'grp'), route)  10.9 us
    all_gather x1, blocking collectives, per_device(): lax.all_gather(block, 'grp', axis=0, tiled=True, axis_index_groups=halves)  10 us
    all_gather x1, blocking collectives, per_device(): both = lax.all_gather(packed, 'grp', axis=0, axis_index_groups=chips)  1.79 us
    pallas_call x1, Pallas kernels, per_device(): call(last_kernel, tile, 64, GRP)  1.25 us
    pallas_call x1, Pallas kernels, per_device(): before_tile = call(visitor_kernel, tile, 64, GRP)(row_maps, before, weights)  1.18 us
  transfers between devices with their start and end apart: 2, of which 2 were waited for; matrix products, arithmetic and copies ran while one was open for 0% of the time, Pallas kernels for 5%

profile of v4, /device:TPU:1, one launch (start us, length us, event | category | flops | bytes accessed | tf_op | source)
XLA Modules:
  0.0 42.2 jit_solution(11673362967082241908)
XLA Ops:
  0.0 0.0 copy-start
  0.0 15.4 %all_gather.12 = bf16[2,48,128]{2,1,0:T(8,128)(2,1)S(1)} all-gather(bf16[1,48,128]{2,1,0:T(8,128)(2,1)} %bitcast.8), channel_id=1, replica_groups={{0,6},{1,7},{2,4},{3,5},{8,14},{9,15},{10,12},{11,13},{16,22},{17,23},{..., dimensions={0}, use_global_device_ids=true | all-gather | bytes 36864 | tf_op jit(solution)/shard_map/all_gather | solution.py:213
  15.4 10.0 %all_gather.13.block_ref = bf16[8,48,128]{2,1,0:T(8,128)(2,1)S(1)} all-gather(bf16[2,48,128]{2,1,0:T(8,128)(2,1)S(1)} %all_gather.12), channel_id=1, replica_groups={{0,1,2,3},{6,7,4,5},{8,9,10,11},{14,15,12,13},{16,17,18,19},{22,23,20,2..., dimensions={0}, use_global_device_ids=true | all-gather | bytes 122880 | tf_op jit(solution)/shard_map/all_gather | solution.py:214
  25.4 2.8 %collective-permute-start.1 = (bf16[8,48,128]{2,1,0:T(8,128)(2,1)S(1)}, bf16[8,48,128]{2,1,0:T(8,128)(2,1)S(1)}, u32[]{:S(2)}, u32[]{:S(2)}) collective-permute-start(bf16[8,48,128]{2,1,0:T(8,128)(2,1)S(1)} %all_gather.13.block_ref), channel_id=1, source_target_pairs={{752,0},{761,1},{754,2},{763,3},{756,4},{765,5},{758,6},{767,7},{7... | collective-permute-start | bytes 294920 | tf_op jit(solution)/shard_map/ppermute | solution.py:205
  28.2 8.2 %collective-permute-start = (bf16[8,48,128]{2,1,0:T(8,128)(2,1)S(1)}, bf16[8,48,128]{2,1,0:T(8,128)(2,1)S(1)}, u32[]{:S(2)}, u32[]{:S(2)}) collective-permute-start(bf16[8,48,128]{2,1,0:T(8,128)(2,1)S(1)} %all_gather.13.block_ref), channel_id=1, source_target_pairs={{16,0},{9,1},{18,2},{11,3},{20,4},{13,5},{22,6},{15,7},{24,8},{17,... | collective-permute-start | bytes 294920 | tf_op jit(solution)/shard_map/ppermute | solution.py:205
  36.4 0.0 copy-done
  36.4 0.8 %shard_map.28 = (f32[8,128]{1,0:T(8,128)S(1)}, f32[4,9,8,128]{3,2,1,0:T(8,128)S(1)}) custom-call(bf16[8,48,128]{2,1,0:T(8,128)(2,1)S(1)} %all_gather.13.block_ref, bf16[256,256]{1,0:T(8,128)(2,1)S(1)} %copy-done), custom_call_target="tpu_custom_call" | custom-call | flops 50331648 | bytes 1048576 | tf_op jit(solution)/shard_map/pallas_call | solution.py:220
  37.1 0.1 collective-permute-done.1.block_ref
  37.2 1.2 %shard_map.29.before_ref = f32[8,128]{1,0:T(8,128)S(1)} custom-call(f32[4,9,8,128]{3,2,1,0:T(8,128)S(1)} %get-tuple-element.7.rows_ref, bf16[8,48,128]{2,1,0:T(8,128)(2,1)S(1)} %collective-permute-done.1.block_ref, bf16[256,256]{1,0:T(8,128)(2,1)S(1)} %copy-done), custom_call_target="tpu_custom_call" | custom-call | flops 100663296 | bytes 1048576 | tf_op jit(solution)/shard_map/pallas_call | solution.py:221
  38.4 0.2 collective-permute-done.block_ref
  38.5 1.2 %shard_map.30 = f32[8,128]{1,0:T(8,128)S(1)} custom-call(f32[4,9,8,128]{3,2,1,0:T(8,128)S(1)} %get-tuple-element.7.rows_ref, bf16[8,48,128]{2,1,0:T(8,128)(2,1)S(1)} %collective-permute-done.block_ref, bf16[256,256]{1,0:T(8,128)(2,1)S(1)} %copy-done, f32[8,128]{1,0:T(8,128)S(1)} %get-tuple-element.8.own_ref, f32[8,128]{1,0:T(8,128)S(1)} %shard_map.29.before_ref), custom_call_target="tpu_custom_call" | custom-call | flops 100663296 | bytes 1048576 | tf_op jit(solution)/shard_map/pallas_call | solution.py:222
  39.8 1.8 %all-gather = f32[16,128]{1,0:T(8,128)S(1)} all-gather(f32[8,128]{1,0:T(8,128)S(1)} %shard_map.30), channel_id=2, replica_groups={{0,1},{2,3},{4,5},{6,7},{8,9},{10,11},{12,13},{14,15},{16,17},{18,19},{..., dimensions={0}, use_global_device_ids=true | all-gather | bytes 12288 | tf_op jit(solution)/shard_map/all_gather | solution.py:224
  41.6 0.7 %shard_map.31 = f32[5,2,16]{2,1,0:T(2,128)} custom-call(f32[2,8,128]{2,1,0:T(8,128)S(1)} %bitcast.7), custom_call_target="tpu_custom_call" | custom-call | bytes 1048576 | tf_op jit(solution)/shard_map/pallas_call | solution.py:225
Async XLA Ops:
  0.0 36.4 %copy-start = (bf16[256,256]{1,0:T(8,128)(2,1)S(1)}, bf16[256,256]{1,0:T(8,128)(2,1)}, u32[]{:S(2)}) copy-start(bf16[256,256]{1,0:T(8,128)(2,1)} %constant.2.clone.weights_ref) | copy-start | bytes 393220
  25.4 11.8 %collective-permute-start.1 = (bf16[8,48,128]{2,1,0:T(8,128)(2,1)S(1)}, bf16[8,48,128]{2,1,0:T(8,128)(2,1)S(1)}, u32[]{:S(2)}, u32[]{:S(2)}) collective-permute-start(bf16[8,48,128]{2,1,0:T(8,128)(2,1)S(1)} %all_gather.13.block_ref), channel_id=1, source_target_pairs={{752,0},{761,1},{754,2},{763,3},{756,4},{765,5},{758,6},{767,7},{7... | collective-permute-start | bytes 294920 | tf_op jit(solution)/shard_map/ppermute | solution.py:205
  28.2 10.4 %collective-permute-start = (bf16[8,48,128]{2,1,0:T(8,128)(2,1)S(1)}, bf16[8,48,128]{2,1,0:T(8,128)(2,1)S(1)}, u32[]{:S(2)}, u32[]{:S(2)}) collective-permute-start(bf16[8,48,128]{2,1,0:T(8,128)(2,1)S(1)} %all_gather.13.block_ref), channel_id=1, source_target_pairs={{16,0},{9,1},{18,2},{11,3},{20,4},{13,5},{22,6},{15,7},{24,8},{17,... | collective-permute-start | bytes 294920 | tf_op jit(solution)/shard_map/ppermute | solution.py:205

commit v5 on v4

--- a/solution.py
+++ b/solution.py
@@ -169,18 +169,16 @@
 
 
 def last_kernel(rows_ref, block_ref, weights_ref, own_ref, before_ref, tile_ref, spread):
-    after = visitor_tile(rows_ref, block_ref, weights_ref, spread)
-    tile_ref[...] = own_ref[...] + pltpu.roll(before_ref[...], 8, 1) + pltpu.roll(after, 24, 1)
-
-
-def assemble_kernel(both_ref, out_ref):
     core = lax.axis_index("grp") % 2
-    low, high = [jnp.where(core == 0, both_ref[at, :2], both_ref[at, 2:4]) for at in (0, 1)]
-    out_ref[0] = low[:, 8:24]
-    out_ref[1] = high[:, 8:24]
-    out_ref[2] = jnp.concatenate([low[:, :8], high[:, :8]], 1)
-    out_ref[3] = high[:, 24:40]
-    out_ref[4] = low[:, 24:40]
+    after = visitor_tile(rows_ref, block_ref, weights_ref, spread)[:CHIP_ROWS, :16]
+    before = before_ref[:CHIP_ROWS, :16]
+    own = own_ref[...]
+    own = jnp.where(core == 0, own, pltpu.roll(own, 8, 1))[:CHIP_ROWS, :16]
+    tile_ref[0] = jnp.where(core == 0, before, 0.0)
+    tile_ref[1] = jnp.where(core == 0, 0.0, before)
+    tile_ref[2] = own
+    tile_ref[3] = jnp.where(core == 0, 0.0, after)
+    tile_ref[4] = jnp.where(core == 0, after, 0.0)
 
 
 def call(body, outs, pairs, places):
@@ -219,10 +217,12 @@
     rows = jax.ShapeDtypeStruct((CHIP_ROWS, 9, 8, 128), jnp.float32)
     own_tile, row_maps = call(own_kernel, (tile, rows), 32, 6)(block, weights)
     before_tile = call(visitor_kernel, tile, 64, GRP)(row_maps, before, weights)
-    packed = call(last_kernel, tile, 64, GRP)(row_maps, after, weights, own_tile, before_tile)
+    span = jax.ShapeDtypeStruct((5, CHIP_ROWS, 16), jnp.float32)
+    packed = call(last_kernel, span, 64, GRP)(row_maps, after, weights, own_tile, before_tile)
     chips = [[2 * chip, 2 * chip + 1] for chip in range(GRP // 2)]
     both = lax.all_gather(packed, "grp", axis=0, axis_index_groups=chips)
-    result = call(assemble_kernel, jax.ShapeDtypeStruct((5, 2, 16), jnp.float32), 0, 0)(both)
+    first = lax.axis_index("grp") % 2 == 0
+    result = jnp.where(first, both[0, :, :2] + both[1, :, :2], both[0, :, 2:] + both[1, :, 2:])
     return jnp.transpose(result, (1, 0, 2))
 
 

time: 42.4 us -> 42.3 us (level)
  Pallas kernels: 3.86 us -> 3.11 us
  other arithmetic: 0 us -> 0.6 us
    pallas_call x2 -> x1, Pallas kernels: 1.92 us -> 1.17 us  [per_device(): call(last_kernel, span, 64, GRP)]
    transpose x0 -> x1, other arithmetic: none -> 0.6 us  [per_device(): return jnp.transpose(result, (1, 0, 2))]
where the time goes in v5:
time: 42.3 us; the launch traced here: 42.1 us
  blocking collectives  27.2 us (64%)
  starting transfers between devices  10.9 us (26%)
  Pallas kernels  3.11 us (7%)
  other arithmetic  0.6 us (1%)
    all_gather x1, blocking collectives, per_device(): lax.all_gather(mine, 'grp', axis=0, tiled=True, axis_index_groups=pairs)  15.4 us
    ppermute x2, starting transfers between devices, by_core(): return lax.ppermute(block, ('blk', 'grp'), route)  10.9 us
    all_gather x1, blocking collectives, per_device(): lax.all_gather(block, 'grp', axis=0, tiled=True, axis_index_groups=halves)  10 us
    all_gather x1, blocking collectives, per_device(): both = lax.all_gather(packed, 'grp', axis=0, axis_index_groups=chips)  1.82 us
    pallas_call x1, Pallas kernels, per_device(): call(last_kernel, span, 64, GRP)  1.17 us
    pallas_call x1, Pallas kernels, per_device(): before_tile = call(visitor_kernel, tile, 64, GRP)(row_maps, before, weights)  1.17 us
  transfers between devices with their start and end apart: 2, of which 2 were waited for; matrix products, arithmetic and copies ran while one was open for 0% of the time, Pallas kernels for 5%

profile of v5, /device:TPU:1, one launch (start us, length us, event | category | flops | bytes accessed | tf_op | source)
XLA Modules:
  0.0 42.1 jit_solution(14984351336614446344)
XLA Ops:
  0.0 0.0 copy-start
  0.0 15.4 %all_gather.12 = bf16[2,48,128]{2,1,0:T(8,128)(2,1)S(1)} all-gather(bf16[1,48,128]{2,1,0:T(8,128)(2,1)} %bitcast.11), channel_id=1, replica_groups={{0,6},{1,7},{2,4},{3,5},{8,14},{9,15},{10,12},{11,13},{16,22},{17,23},{..., dimensions={0}, use_global_device_ids=true | all-gather | bytes 36864 | tf_op jit(solution)/shard_map/all_gather | solution.py:211
  15.4 10.0 %all_gather.13.block_ref = bf16[8,48,128]{2,1,0:T(8,128)(2,1)S(1)} all-gather(bf16[2,48,128]{2,1,0:T(8,128)(2,1)S(1)} %all_gather.12), channel_id=1, replica_groups={{0,1,2,3},{6,7,4,5},{8,9,10,11},{14,15,12,13},{16,17,18,19},{22,23,20,2..., dimensions={0}, use_global_device_ids=true | all-gather | bytes 122880 | tf_op jit(solution)/shard_map/all_gather | solution.py:212
  25.4 2.8 %collective-permute-start.1 = (bf16[8,48,128]{2,1,0:T(8,128)(2,1)S(1)}, bf16[8,48,128]{2,1,0:T(8,128)(2,1)S(1)}, u32[]{:S(2)}, u32[]{:S(2)}) collective-permute-start(bf16[8,48,128]{2,1,0:T(8,128)(2,1)S(1)} %all_gather.13.block_ref), channel_id=1, source_target_pairs={{752,0},{761,1},{754,2},{763,3},{756,4},{765,5},{758,6},{767,7},{7... | collective-permute-start | bytes 294920 | tf_op jit(solution)/shard_map/ppermute | solution.py:203
  28.2 8.2 %collective-permute-start = (bf16[8,48,128]{2,1,0:T(8,128)(2,1)S(1)}, bf16[8,48,128]{2,1,0:T(8,128)(2,1)S(1)}, u32[]{:S(2)}, u32[]{:S(2)}) collective-permute-start(bf16[8,48,128]{2,1,0:T(8,128)(2,1)S(1)} %all_gather.13.block_ref), channel_id=1, source_target_pairs={{16,0},{9,1},{18,2},{11,3},{20,4},{13,5},{22,6},{15,7},{24,8},{17,... | collective-permute-start | bytes 294920 | tf_op jit(solution)/shard_map/ppermute | solution.py:203
  36.4 0.0 copy-done
  36.4 0.8 %shard_map.28 = (f32[8,128]{1,0:T(8,128)S(1)}, f32[4,9,8,128]{3,2,1,0:T(8,128)S(1)}) custom-call(bf16[8,48,128]{2,1,0:T(8,128)(2,1)S(1)} %all_gather.13.block_ref, bf16[256,256]{1,0:T(8,128)(2,1)S(1)} %copy-done), custom_call_target="tpu_custom_call" | custom-call | flops 50331648 | bytes 1048576 | tf_op jit(solution)/shard_map/pallas_call | solution.py:218
  37.1 0.1 collective-permute-done.1.block_ref
  37.2 1.2 %shard_map.29.before_ref = f32[8,128]{1,0:T(8,128)S(1)} custom-call(f32[4,9,8,128]{3,2,1,0:T(8,128)S(1)} %get-tuple-element.7.rows_ref, bf16[8,48,128]{2,1,0:T(8,128)(2,1)S(1)} %collective-permute-done.1.block_ref, bf16[256,256]{1,0:T(8,128)(2,1)S(1)} %copy-done), custom_call_target="tpu_custom_call" | custom-call | flops 100663296 | bytes 1048576 | tf_op jit(solution)/shard_map/pallas_call | solution.py:219
  38.4 0.2 collective-permute-done.block_ref
  38.5 1.2 %shard_map.30 = f32[5,4,16]{2,1,0:T(4,128)S(1)} custom-call(f32[4,9,8,128]{3,2,1,0:T(8,128)S(1)} %get-tuple-element.7.rows_ref, bf16[8,48,128]{2,1,0:T(8,128)(2,1)S(1)} %collective-permute-done.block_ref, bf16[256,256]{1,0:T(8,128)(2,1)S(1)} %copy-done, f32[8,128]{1,0:T(8,128)S(1)} %get-tuple-element.8.own_ref, f32[8,128]{1,0:T(8,128)S(1)} %shard_map.29.before_ref), custom_call_target="tpu_custom_call" | custom-call | flops 100663296 | bytes 1048576 | tf_op jit(solution)/shard_map/pallas_call | solution.py:221
  39.7 1.8 %all-gather = f32[10,4,16]{2,1,0:T(4,128)S(1)} all-gather(f32[5,4,16]{2,1,0:T(4,128)S(1)} %shard_map.30), channel_id=2, replica_groups={{0,1},{2,3},{4,5},{6,7},{8,9},{10,11},{12,13},{14,15},{16,17},{18,19},{..., dimensions={0}, use_global_device_ids=true | all-gather | bytes 3840 | tf_op jit(solution)/shard_map/all_gather | solution.py:223
  41.5 0.6 %fusion.1 = f32[2,5,16]{2,0,1:T(2,128)} fusion(f32[2,5,4,16]{3,2,1,0:T(4,128)S(1)} %bitcast.10, pred[]{:T(512)S(6)} %eq.5), kind=kLoop, calls=%fused_computation.2 | loop fusion | flops 480 | bytes 3201 | tf_op jit(solution)/shard_map/transpose | solution.py:226
Async XLA Ops:
  0.0 36.4 %copy-start = (bf16[256,256]{1,0:T(8,128)(2,1)S(1)}, bf16[256,256]{1,0:T(8,128)(2,1)}, u32[]{:S(2)}) copy-start(bf16[256,256]{1,0:T(8,128)(2,1)} %constant.20.clone.weights_ref) | copy-start | bytes 393220
  25.4 11.8 %collective-permute-start.1 = (bf16[8,48,128]{2,1,0:T(8,128)(2,1)S(1)}, bf16[8,48,128]{2,1,0:T(8,128)(2,1)S(1)}, u32[]{:S(2)}, u32[]{:S(2)}) collective-permute-start(bf16[8,48,128]{2,1,0:T(8,128)(2,1)S(1)} %all_gather.13.block_ref), channel_id=1, source_target_pairs={{752,0},{761,1},{754,2},{763,3},{756,4},{765,5},{758,6},{767,7},{7... | collective-permute-start | bytes 294920 | tf_op jit(solution)/shard_map/ppermute | solution.py:203
  28.2 10.4 %collective-permute-start = (bf16[8,48,128]{2,1,0:T(8,128)(2,1)S(1)}, bf16[8,48,128]{2,1,0:T(8,128)(2,1)S(1)}, u32[]{:S(2)}, u32[]{:S(2)}) collective-permute-start(bf16[8,48,128]{2,1,0:T(8,128)(2,1)S(1)} %all_gather.13.block_ref), channel_id=1, source_target_pairs={{16,0},{9,1},{18,2},{11,3},{20,4},{13,5},{22,6},{15,7},{24,8},{17,... | collective-permute-start | bytes 294920 | tf_op jit(solution)/shard_map/ppermute | solution.py:203

commit v6 on v5

--- a/solution.py
+++ b/solution.py
@@ -86,7 +86,9 @@
 
 def fold(maps):
     sub = lax.broadcasted_iota(jnp.int32, (1, 8, 128), 1)
-    for width in (4, 2, 1):
+    if maps.shape[0] == 4:
+        maps = maps + pltpu.roll(maps, 4, 1)
+    for width in (4, 2, 1)[8 // maps.shape[0] - 1 :]:
         first, second = maps[:width], maps[width:]
         low = (sub % (2 * width)) < width
         kept = jnp.where(low, first, second)
@@ -108,11 +110,11 @@
     pairs = CHIP_ROWS * count
     maps = []
     for row in range(CHIP_ROWS):
-        terms = (row_channels[row] * (1.0 / 27.0))[None] * columns
+        terms = row_channels[row][None] * columns
         maps.append(terms[:, 0] + terms[:, 1] + terms[:, 2])
     squared = squares(columns)
     if row_maps is None:
-        squared = jnp.concatenate([squared, squares(row_channels)], 0)
+        squared = jnp.concatenate([squared, squares(row_channels) * 729.0], 0)
     made = []
     for layer in range(LAYERS):
         variance = stencil_sum(squared, weights, above, below) + bias_var
@@ -138,7 +140,6 @@
             total = jnp.sum(fold(maps[row][group : group + 8]), 1, keepdims=True)
             spot = jnp.where(lane == sub + group, total, spot)
         spots.append(spot)
-    spots += [jnp.zeros((8, 128), jnp.float32)] * (8 - CHIP_ROWS)
     tile = fold(jnp.stack(spots, 0))
     return tile, made
 
@@ -147,7 +148,7 @@
     place = lax.axis_index("grp")
     chip, core = place // 2, place % 2
     at = jnp.where(chip == 0, 0, jnp.where(chip == 1, 4, jnp.where(chip == 2, 5, 1)))
-    rows = load_images(block_ref, (at, at + 2), spread)
+    rows = load_images(block_ref, (at, at + 2), spread) * (1.0 / 27.0)
     half = [jnp.where(core == 0, ORDER[n], ORDER[n + 4]) for n in range(4)]
     columns = load_images(block_ref, half, spread, 2)
     tile, row_maps = pair_tile(rows, columns, weights_ref[...])

time: 42.3 us -> 42.3 us (level)
  no operation moved by 1% of the time
where the time goes in v6:
time: 42.3 us; the launch traced here: 42.1 us
  blocking collectives  27.2 us (64%)
  starting transfers between devices  10.9 us (26%)
  Pallas kernels  3.09 us (7%)
  other arithmetic  0.6 us (1%)
    all_gather x1, blocking collectives, per_device(): lax.all_gather(mine, 'grp', axis=0, tiled=True, axis_index_groups=pairs)  15.4 us
    ppermute x2, starting transfers between devices, by_core(): return lax.ppermute(block, ('blk', 'grp'), route)  10.9 us
    all_gather x1, blocking collectives, per_device(): lax.all_gather(block, 'grp', axis=0, tiled=True, axis_index_groups=halves)  10 us
    all_gather x1, blocking collectives, per_device(): both = lax.all_gather(packed, 'grp', axis=0, axis_index_groups=chips)  1.81 us
    pallas_call x1, Pallas kernels, per_device(): call(last_kernel, span, 64, GRP)  1.17 us
    pallas_call x1, Pallas kernels, per_device(): before_tile = call(visitor_kernel, tile, 64, GRP)(row_maps, before, weights)  1.16 us
  transfers between devices with their start and end apart: 2, of which 2 were waited for; matrix products, arithmetic and copies ran while one was open for 0% of the time, Pallas kernels for 5%

profile of v6, /device:TPU:1, one launch (start us, length us, event | category | flops | bytes accessed | tf_op | source)
XLA Modules:
  0.0 42.1 jit_solution(12696922820435985377)
XLA Ops:
  0.0 0.0 copy-start
  0.0 15.4 %all_gather.12 = bf16[2,48,128]{2,1,0:T(8,128)(2,1)S(1)} all-gather(bf16[1,48,128]{2,1,0:T(8,128)(2,1)} %bitcast.11), channel_id=1, replica_groups={{0,6},{1,7},{2,4},{3,5},{8,14},{9,15},{10,12},{11,13},{16,22},{17,23},{..., dimensions={0}, use_global_device_ids=true | all-gather | bytes 36864 | tf_op jit(solution)/shard_map/all_gather | solution.py:212
  15.4 10.0 %all_gather.13.block_ref = bf16[8,48,128]{2,1,0:T(8,128)(2,1)S(1)} all-gather(bf16[2,48,128]{2,1,0:T(8,128)(2,1)S(1)} %all_gather.12), channel_id=1, replica_groups={{0,1,2,3},{6,7,4,5},{8,9,10,11},{14,15,12,13},{16,17,18,19},{22,23,20,2..., dimensions={0}, use_global_device_ids=true | all-gather | bytes 122880 | tf_op jit(solution)/shard_map/all_gather | solution.py:213
  25.4 2.8 %collective-permute-start.1 = (bf16[8,48,128]{2,1,0:T(8,128)(2,1)S(1)}, bf16[8,48,128]{2,1,0:T(8,128)(2,1)S(1)}, u32[]{:S(2)}, u32[]{:S(2)}) collective-permute-start(bf16[8,48,128]{2,1,0:T(8,128)(2,1)S(1)} %all_gather.13.block_ref), channel_id=1, source_target_pairs={{752,0},{761,1},{754,2},{763,3},{756,4},{765,5},{758,6},{767,7},{7... | collective-permute-start | bytes 294920 | tf_op jit(solution)/shard_map/ppermute | solution.py:204
  28.2 8.2 %collective-permute-start = (bf16[8,48,128]{2,1,0:T(8,128)(2,1)S(1)}, bf16[8,48,128]{2,1,0:T(8,128)(2,1)S(1)}, u32[]{:S(2)}, u32[]{:S(2)}) collective-permute-start(bf16[8,48,128]{2,1,0:T(8,128)(2,1)S(1)} %all_gather.13.block_ref), channel_id=1, source_target_pairs={{16,0},{9,1},{18,2},{11,3},{20,4},{13,5},{22,6},{15,7},{24,8},{17,... | collective-permute-start | bytes 294920 | tf_op jit(solution)/shard_map/ppermute | solution.py:204
  36.4 0.0 copy-done
  36.4 0.8 %shard_map.28 = (f32[8,128]{1,0:T(8,128)S(1)}, f32[4,9,8,128]{3,2,1,0:T(8,128)S(1)}) custom-call(bf16[8,48,128]{2,1,0:T(8,128)(2,1)S(1)} %all_gather.13.block_ref, bf16[256,256]{1,0:T(8,128)(2,1)S(1)} %copy-done), custom_call_target="tpu_custom_call" | custom-call | flops 50331648 | bytes 1048576 | tf_op jit(solution)/shard_map/pallas_call | solution.py:219
  37.1 0.1 collective-permute-done.1.block_ref
  37.2 1.2 %shard_map.29.before_ref = f32[8,128]{1,0:T(8,128)S(1)} custom-call(f32[4,9,8,128]{3,2,1,0:T(8,128)S(1)} %get-tuple-element.7.rows_ref, bf16[8,48,128]{2,1,0:T(8,128)(2,1)S(1)} %collective-permute-done.1.block_ref, bf16[256,256]{1,0:T(8,128)(2,1)S(1)} %copy-done), custom_call_target="tpu_custom_call" | custom-call | flops 100663296 | bytes 1048576 | tf_op jit(solution)/shard_map/pallas_call | solution.py:220
  38.4 0.2 collective-permute-done.block_ref
  38.5 1.2 %shard_map.30 = f32[5,4,16]{2,1,0:T(4,128)S(1)} custom-call(f32[4,9,8,128]{3,2,1,0:T(8,128)S(1)} %get-tuple-element.7.rows_ref, bf16[8,48,128]{2,1,0:T(8,128)(2,1)S(1)} %collective-permute-done.block_ref, bf16[256,256]{1,0:T(8,128)(2,1)S(1)} %copy-done, f32[8,128]{1,0:T(8,128)S(1)} %get-tuple-element.8.own_ref, f32[8,128]{1,0:T(8,128)S(1)} %shard_map.29.before_ref), custom_call_target="tpu_custom_call" | custom-call | flops 100663296 | bytes 1048576 | tf_op jit(solution)/shard_map/pallas_call | solution.py:222
  39.7 1.8 %all-gather = f32[10,4,16]{2,1,0:T(4,128)S(1)} all-gather(f32[5,4,16]{2,1,0:T(4,128)S(1)} %shard_map.30), channel_id=2, replica_groups={{0,1},{2,3},{4,5},{6,7},{8,9},{10,11},{12,13},{14,15},{16,17},{18,19},{..., dimensions={0}, use_global_device_ids=true | all-gather | bytes 3840 | tf_op jit(solution)/shard_map/all_gather | solution.py:224
  41.5 0.6 %fusion.1 = f32[2,5,16]{2,0,1:T(2,128)} fusion(f32[2,5,4,16]{3,2,1,0:T(4,128)S(1)} %bitcast.10, pred[]{:T(512)S(6)} %eq.5), kind=kLoop, calls=%fused_computation.2 | loop fusion | flops 480 | bytes 3201 | tf_op jit(solution)/shard_map/transpose | solution.py:227
Async XLA Ops:
  0.0 36.4 %copy-start = (bf16[256,256]{1,0:T(8,128)(2,1)S(1)}, bf16[256,256]{1,0:T(8,128)(2,1)}, u32[]{:S(2)}) copy-start(bf16[256,256]{1,0:T(8,128)(2,1)} %constant.20.clone.weights_ref) | copy-start | bytes 393220
  25.4 11.8 %collective-permute-start.1 = (bf16[8,48,128]{2,1,0:T(8,128)(2,1)S(1)}, bf16[8,48,128]{2,1,0:T(8,128)(2,1)S(1)}, u32[]{:S(2)}, u32[]{:S(2)}) collective-permute-start(bf16[8,48,128]{2,1,0:T(8,128)(2,1)S(1)} %all_gather.13.block_ref), channel_id=1, source_target_pairs={{752,0},{761,1},{754,2},{763,3},{756,4},{765,5},{758,6},{767,7},{7... | collective-permute-start | bytes 294920 | tf_op jit(solution)/shard_map/ppermute | solution.py:204
  28.2 10.4 %collective-permute-start = (bf16[8,48,128]{2,1,0:T(8,128)(2,1)S(1)}, bf16[8,48,128]{2,1,0:T(8,128)(2,1)S(1)}, u32[]{:S(2)}, u32[]{:S(2)}) collective-permute-start(bf16[8,48,128]{2,1,0:T(8,128)(2,1)S(1)} %all_gather.13.block_ref), channel_id=1, source_target_pairs={{16,0},{9,1},{18,2},{11,3},{20,4},{13,5},{22,6},{15,7},{24,8},{17,... | collective-permute-start | bytes 294920 | tf_op jit(solution)/shard_map/ppermute | solution.py:204

commit v7 on v6

--- a/solution.py
+++ b/solution.py
@@ -200,7 +200,10 @@
         for place in range(GRP):
             step = place % 2 + 1 if nearer else 2 - place % 2
             source = (block_index + direction * step) % blocks
-            route.append((source * GRP + place, block_index * GRP + place))
+            sender = place
+            if direction > 0 and (block_index % 3, place) in ((2, 1), (1, 2)):
+                sender = 3 - place
+            route.append((source * GRP + sender, block_index * GRP + place))
     return lax.ppermute(block, ("blk", "grp"), route)
 
 

time: 42.3 us -> 42.3 us (level)
  starting transfers between devices: 10.9 us -> 10.4 us
    ppermute x2, starting transfers between devices: 10.9 us -> 10.4 us  [by_core(): return lax.ppermute(block, ('blk', 'grp'), route)]
  transfers between devices with their start and end apart: 2 -> 2, of which waited for: 2 -> 1; matrix products, arithmetic and copies ran while one was open for 0% -> 0% of each run, Pallas kernels for 5% -> 5%
where the time goes in v7:
time: 42.3 us; the launch traced here: 42.1 us
  blocking collectives  27.3 us (65%)
  starting transfers between devices  10.4 us (25%)
  Pallas kernels  3.1 us (7%)
  other arithmetic  0.6 us (1%)
  waiting for transfers between devices  0.59 us (1%)
    all_gather x1, blocking collectives, per_device(): lax.all_gather(mine, 'grp', axis=0, tiled=True, axis_index_groups=pairs)  15.4 us
    ppermute x2, starting transfers between devices, by_core(): return lax.ppermute(block, ('blk', 'grp'), route)  10.4 us
    all_gather x1, blocking collectives, per_device(): lax.all_gather(block, 'grp', axis=0, tiled=True, axis_index_groups=halves)  10 us
    all_gather x1, blocking collectives, per_device(): both = lax.all_gather(packed, 'grp', axis=0, axis_index_groups=chips)  1.92 us
    pallas_call x1, Pallas kernels, per_device(): call(last_kernel, span, 64, GRP)  1.17 us
    pallas_call x1, Pallas kernels, per_device(): before_tile = call(visitor_kernel, tile, 64, GRP)(row_maps, before, weights)  1.16 us
  transfers between devices with their start and end apart: 2, of which 1 were waited for; matrix products, arithmetic and copies ran while one was open for 0% of the time, Pallas kernels for 5%

profile of v7, /device:TPU:1, one launch (start us, length us, event | category | flops | bytes accessed | tf_op | source)
XLA Modules:
  0.0 42.1 jit_solution(15378858575055154156)
XLA Ops:
  0.0 0.0 copy-start
  0.0 15.4 %all_gather.12 = bf16[2,48,128]{2,1,0:T(8,128)(2,1)S(1)} all-gather(bf16[1,48,128]{2,1,0:T(8,128)(2,1)} %bitcast.11), channel_id=1, replica_groups={{0,6},{1,7},{2,4},{3,5},{8,14},{9,15},{10,12},{11,13},{16,22},{17,23},{..., dimensions={0}, use_global_device_ids=true | all-gather | bytes 36864 | tf_op jit(solution)/shard_map/all_gather | solution.py:215
  15.4 10.0 %all_gather.13.block_ref = bf16[8,48,128]{2,1,0:T(8,128)(2,1)S(1)} all-gather(bf16[2,48,128]{2,1,0:T(8,128)(2,1)S(1)} %all_gather.12), channel_id=1, replica_groups={{0,1,2,3},{6,7,4,5},{8,9,10,11},{14,15,12,13},{16,17,18,19},{22,23,20,2..., dimensions={0}, use_global_device_ids=true | all-gather | bytes 122880 | tf_op jit(solution)/shard_map/all_gather | solution.py:216
  25.4 2.8 %collective-permute-start.1 = (bf16[8,48,128]{2,1,0:T(8,128)(2,1)S(1)}, bf16[8,48,128]{2,1,0:T(8,128)(2,1)S(1)}, u32[]{:S(2)}, u32[]{:S(2)}) collective-permute-start(bf16[8,48,128]{2,1,0:T(8,128)(2,1)S(1)} %all_gather.13.block_ref), channel_id=1, source_target_pairs={{752,0},{761,1},{754,2},{763,3},{756,4},{765,5},{758,6},{767,7},{7... | collective-permute-start | bytes 294920 | tf_op jit(solution)/shard_map/ppermute | solution.py:207
  28.2 7.7 %collective-permute-start = (bf16[8,48,128]{2,1,0:T(8,128)(2,1)S(1)}, bf16[8,48,128]{2,1,0:T(8,128)(2,1)S(1)}, u32[]{:S(2)}, u32[]{:S(2)}) collective-permute-start(bf16[8,48,128]{2,1,0:T(8,128)(2,1)S(1)} %all_gather.13.block_ref), channel_id=1, source_target_pairs={{16,0},{9,1},{18,2},{11,3},{20,4},{13,5},{22,6},{15,7},{24,8},{17,... | collective-permute-start | bytes 294920 | tf_op jit(solution)/shard_map/ppermute | solution.py:207
  35.9 0.0 copy-done
  35.9 0.8 %shard_map.28 = (f32[8,128]{1,0:T(8,128)S(1)}, f32[4,9,8,128]{3,2,1,0:T(8,128)S(1)}) custom-call(bf16[8,48,128]{2,1,0:T(8,128)(2,1)S(1)} %all_gather.13.block_ref, bf16[256,256]{1,0:T(8,128)(2,1)S(1)} %copy-done), custom_call_target="tpu_custom_call" | custom-call | flops 50331648 | bytes 1048576 | tf_op jit(solution)/shard_map/pallas_call | solution.py:222
  36.6 0.6 %collective-permute-done.1.block_ref = bf16[8,48,128]{2,1,0:T(8,128)(2,1)S(1)} collective-permute-done((bf16[8,48,128]{2,1,0:T(8,128)(2,1)S(1)}, bf16[8,48,128]{2,1,0:T(8,128)(2,1)S(1)}, u32[]{:S(2)}, u32[]{:S(2)}) %collective-permute-start.1) | collective-permute-done | bytes 98336 | tf_op jit(solution)/shard_map/ppermute | solution.py:207
  37.2 1.2 %shard_map.29.before_ref = f32[8,128]{1,0:T(8,128)S(1)} custom-call(f32[4,9,8,128]{3,2,1,0:T(8,128)S(1)} %get-tuple-element.7.rows_ref, bf16[8,48,128]{2,1,0:T(8,128)(2,1)S(1)} %collective-permute-done.1.block_ref, bf16[256,256]{1,0:T(8,128)(2,1)S(1)} %copy-done), custom_call_target="tpu_custom_call" | custom-call | flops 100663296 | bytes 1048576 | tf_op jit(solution)/shard_map/pallas_call | solution.py:223
  38.4 0.0 collective-permute-done.block_ref
  38.4 1.2 %shard_map.30 = f32[5,4,16]{2,1,0:T(4,128)S(1)} custom-call(f32[4,9,8,128]{3,2,1,0:T(8,128)S(1)} %get-tuple-element.7.rows_ref, bf16[8,48,128]{2,1,0:T(8,128)(2,1)S(1)} %collective-permute-done.block_ref, bf16[256,256]{1,0:T(8,128)(2,1)S(1)} %copy-done, f32[8,128]{1,0:T(8,128)S(1)} %get-tuple-element.8.own_ref, f32[8,128]{1,0:T(8,128)S(1)} %shard_map.29.before_ref), custom_call_target="tpu_custom_call" | custom-call | flops 100663296 | bytes 1048576 | tf_op jit(solution)/shard_map/pallas_call | solution.py:225
  39.6 1.9 %all-gather = f32[10,4,16]{2,1,0:T(4,128)S(1)} all-gather(f32[5,4,16]{2,1,0:T(4,128)S(1)} %shard_map.30), channel_id=2, replica_groups={{0,1},{2,3},{4,5},{6,7},{8,9},{10,11},{12,13},{14,15},{16,17},{18,19},{..., dimensions={0}, use_global_device_ids=true | all-gather | bytes 3840 | tf_op jit(solution)/shard_map/all_gather | solution.py:227
  41.5 0.6 %fusion.1 = f32[2,5,16]{2,0,1:T(2,128)} fusion(f32[2,5,4,16]{3,2,1,0:T(4,128)S(1)} %bitcast.10, pred[]{:T(512)S(6)} %eq.5), kind=kLoop, calls=%fused_computation.2 | loop fusion | flops 480 | bytes 3201 | tf_op jit(solution)/shard_map/transpose | solution.py:230
Async XLA Ops:
  0.0 35.9 %copy-start = (bf16[256,256]{1,0:T(8,128)(2,1)S(1)}, bf16[256,256]{1,0:T(8,128)(2,1)}, u32[]{:S(2)}) copy-start(bf16[256,256]{1,0:T(8,128)(2,1)} %constant.20.clone.weights_ref) | copy-start | bytes 393220
  25.4 11.8 %collective-permute-start.1 = (bf16[8,48,128]{2,1,0:T(8,128)(2,1)S(1)}, bf16[8,48,128]{2,1,0:T(8,128)(2,1)S(1)}, u32[]{:S(2)}, u32[]{:S(2)}) collective-permute-start(bf16[8,48,128]{2,1,0:T(8,128)(2,1)S(1)} %all_gather.13.block_ref), channel_id=1, source_target_pairs={{752,0},{761,1},{754,2},{763,3},{756,4},{765,5},{758,6},{767,7},{7... | collective-permute-start | bytes 294920 | tf_op jit(solution)/shard_map/ppermute | solution.py:207
  28.2 10.2 %collective-permute-start = (bf16[8,48,128]{2,1,0:T(8,128)(2,1)S(1)}, bf16[8,48,128]{2,1,0:T(8,128)(2,1)S(1)}, u32[]{:S(2)}, u32[]{:S(2)}) collective-permute-start(bf16[8,48,128]{2,1,0:T(8,128)(2,1)S(1)} %all_gather.13.block_ref), channel_id=1, source_target_pairs={{16,0},{9,1},{18,2},{11,3},{20,4},{13,5},{22,6},{15,7},{24,8},{17,... | collective-permute-start | bytes 294920 | tf_op jit(solution)/shard_map/ppermute | solution.py:207
